TPU v7x, 512 devices: a whole 4x8x8 slice. The times are simulated.
512 devices in a mesh: angle: 16 (over y, core), tile: 32 (over x, z).
Axes of the slice: x: 4, y: 8, z: 8, core: 2. Of those that a mesh axis runs over, the one named last changes fastest.
Arguments:
- patches: bfloat16 [16, 256, 2, 128, 128], P('angle', 'tile'), may hold values from -6 to 6
- magnitudes: bfloat16 [16, 2048, 128, 128], P('angle', 'tile'), may hold values from 0.099609375 to 3
- probe: float32 [2, 128, 128], replicated, may hold values from -6 to 6
- owners: int32 [16, 256, 1], P('angle', 'tile'), may hold values from 0 to 31; in each aligned block of 8 rows (0 to 7, 8 to 15, ..., all dimensions but the last counted through in order) at most 2 rows name the same one
- scan_rows: int32 [16, 256], P('angle', 'tile'), may hold values from 0 to 384
- scan_cols: int32 [16, 256], P('angle', 'tile'), may hold values from 0 to 896
- slab_rows: int32 [32, 16], P('tile'), may hold values from 0 to 2, as said below
- angle_tan: float32 [16], replicated, may hold values from -0.4 to 0.4
- prior_in: bfloat16 [16, 1, 3, 3], replicated, may hold values from -2 to 2
- prior_out: bfloat16 [1, 16, 3, 3], replicated, may hold values from -0.5 to 0.5
Outputs:
- volume: float32 [32, 32, 16, 1024], P('tile', 'angle')
Inputs may be any that keep to these rules, and one draw needn't show every extreme that they name: `owners`: in the patches of one device, no owner is named by more than 2, and in some devices one owner is named exactly 2 times. Each row of slab_rows sums to 16, and in every row some slab has exactly 2 rows.
All inputs are finite; a program needn't handle non-finite values.
Results may differ from a plain program's by a relative error of at most 0.022.
Values may be sent and summed in bfloat16 or wider, within the bound.
A program may use at most 64 MiB of HBM per device.

v0:
```python
import math

import jax
import jax.numpy as jnp
from jax import lax
from jax.sharding import PartitionSpec as P

H = 512
W = 1024
XW = 16


def dft_table(side):
    index = jnp.arange(side, dtype=jnp.int32)
    product = index[:, None] * index[None, :] % side
    phase = product.astype(jnp.float32) * (2.0 * math.pi / side)
    scale = 1.0 / math.sqrt(side)
    real = jnp.cos(phase) * scale
    imag = -jnp.sin(phase) * scale
    upper = jnp.concatenate([real, imag], axis=1)
    lower = jnp.concatenate([-imag, real], axis=1)
    return jnp.concatenate([upper, lower], axis=0).astype(jnp.bfloat16)


def correct_all(waves, measured, table):
    number = waves.shape[0]
    side = waves.shape[2]
    left = table.T
    joined = jnp.concatenate([waves[:, 0], waves[:, 1]], axis=2).reshape(number * side, 2 * side)
    half = jnp.dot(joined, table, preferred_element_type=jnp.float32).astype(jnp.bfloat16)
    half = half.reshape(number, side, 2 * side)
    stacked = jnp.concatenate([half[:, :, :side], half[:, :, side:]], axis=1)
    stacked = jnp.transpose(stacked, (1, 0, 2)).reshape(2 * side, number * side)
    spectrum = jnp.dot(left, stacked, preferred_element_type=jnp.float32).reshape(
        2 * side, number, side
    )
    real_part = spectrum[:side]
    imag_part = spectrum[side:]
    level = jnp.transpose(measured, (1, 0, 2)).astype(jnp.float32)
    factor = level / jnp.sqrt(real_part * real_part + imag_part * imag_part + 0.25)
    target = jnp.concatenate([real_part * factor, imag_part * factor], axis=2).astype(jnp.bfloat16)
    back = jnp.dot(
        target.reshape(side * number, 2 * side), left, preferred_element_type=jnp.float32
    )
    back = back.astype(jnp.bfloat16).reshape(side, number, 2 * side)
    stacked_back = jnp.concatenate([back[:, :, :side], back[:, :, side:]], axis=0).reshape(
        2 * side, number * side
    )
    result = jnp.dot(table, stacked_back, preferred_element_type=jnp.float32).reshape(
        2, side, number, side
    )
    return jnp.transpose(result, (2, 0, 1, 3)).astype(jnp.bfloat16)


def backproject(sino, angle_tan, width):
    count = sino.shape[1]
    offsets = jnp.arange(XW, dtype=jnp.float32) - (XW - 1) / 2.0
    spread_cols = int(0.2 * (XW - 1)) + 2
    shifts = jnp.arange(-spread_cols, spread_cols + 1, dtype=jnp.int32).astype(jnp.float32)

    def add_angle(total, item):
        rows, tangent = item
        shifted = offsets * tangent
        floor_shift = jnp.floor(shifted)
        fraction = shifted - floor_shift
        low_hit = (shifts[None, :] == floor_shift[:, None]).astype(jnp.float32)
        high_hit = (shifts[None, :] == floor_shift[:, None] + 1.0).astype(jnp.float32)
        weights = (1.0 - fraction)[:, None] * low_hit + fraction[:, None] * high_hit
        padded = jnp.pad(rows, ((0, 0), (spread_cols, spread_cols)))
        columns_stack = jnp.stack(
            [padded[:, step : step + width] for step in range(2 * spread_cols + 1)], axis=0
        )
        term = jnp.einsum("is,scj->cij", weights, columns_stack, precision=lax.Precision.HIGHEST)
        return (total + term, None)

    start = jnp.zeros((count, XW, width), jnp.float32)
    total, unused = lax.scan(add_angle, start, (sino, angle_tan))
    return total / sino.shape[0]


def prior(slices, prior_in, prior_out):
    numbers = ("NCHW", "OIHW", "NCHW")
    rounded = slices.astype(jnp.bfloat16)[:, None].astype(jnp.float32)
    hidden = lax.conv_general_dilated(
        rounded, prior_in.astype(jnp.float32), (1, 1), "SAME", dimension_numbers=numbers
    )
    hidden = jnp.maximum(hidden, 0.0).astype(jnp.bfloat16).astype(jnp.float32)
    extra = lax.conv_general_dilated(
        hidden, prior_out.astype(jnp.float32), (1, 1), "SAME", dimension_numbers=numbers
    )
    return slices + extra[:, 0]


def body(
    patches,
    magnitudes,
    probe,
    owners,
    scan_rows,
    scan_cols,
    slab_rows,
    angle_tan,
    prior_in,
    prior_out,
):
    tiles = lax.axis_size("tile")
    angles = lax.axis_size("angle")
    count = patches.shape[1]
    side = patches.shape[3]
    slots = magnitudes.shape[1]
    depth = slots // tiles
    table = dft_table(side)
    owner = owners[0, :, 0]
    member = (owner[:, None] == jnp.arange(tiles, dtype=jnp.int32)[None, :]).astype(jnp.int32)
    before = jnp.sum((jnp.cumsum(member, axis=0) - member) * member, axis=1)
    slot = owner * depth + before
    select = (jnp.arange(slots, dtype=jnp.int32)[:, None] == slot[None, :]).astype(jnp.bfloat16)
    waves = patches[0]
    packed = jnp.dot(select, waves.reshape(count, -1), preferred_element_type=jnp.float32).astype(
        jnp.bfloat16
    )
    arrived = lax.all_to_all(
        packed.reshape(tiles, depth, 2, side, side), "tile", split_axis=0, concat_axis=0, tiled=True
    )
    fixed = correct_all(arrived.reshape(slots, 2, side, side), magnitudes[0], table)
    returned = lax.all_to_all(
        fixed.reshape(tiles, depth, 2, side, side), "tile", split_axis=0, concat_axis=0, tiled=True
    )
    mine = jnp.dot(select.T, returned.reshape(slots, -1), preferred_element_type=jnp.float32)
    mine = mine.astype(jnp.bfloat16).reshape(count, 2, side, side)
    mine_float = mine.astype(jnp.float32)
    contrib = (probe[0] * mine_float[:, 1] - probe[1] * mine_float[:, 0]) * 0.25
    rows_here = scan_rows[0]
    cols_here = scan_cols[0]
    width = W

    def place(step, canvas):
        row = rows_here[step]
        col = cols_here[step]
        piece = lax.dynamic_slice(canvas, (row, col), (side, side)) + contrib[step]
        return lax.dynamic_update_slice(canvas, piece, (row, col))

    canvas = lax.fori_loop(0, count, place, jnp.zeros((H, width), jnp.float32))
    strip = lax.psum_scatter(
        canvas.astype(jnp.bfloat16), "tile", scatter_dimension=0, tiled=True
    ).astype(jnp.float32)
    strip_rows = strip.shape[0]
    rowcap = 2 * strip_rows // angles
    lengths = slab_rows[0]
    starts = jnp.cumsum(lengths) - lengths
    within = jnp.arange(rowcap, dtype=jnp.int32)
    index = jnp.clip(starts[:, None] + within[None, :], 0, strip_rows - 1)
    valid = (within[None, :] < lengths[:, None]).astype(jnp.float32)
    outgoing = strip[index] * valid[:, :, None]
    slabs = prior(
        backproject(
            lax.all_to_all(
                outgoing.astype(jnp.bfloat16), "angle", split_axis=0, concat_axis=0, tiled=True
            ).astype(outgoing.dtype),
            angle_tan,
            width,
        ),
        prior_in,
        prior_out,
    )
    return slabs[None]


def solution(mesh):
    placed = (
        P("angle", "tile", None, None, None),
        P("angle", "tile", None, None),
        P(),
        P("angle", "tile", None),
        P("angle", "tile"),
        P("angle", "tile"),
        P("tile", None),
        P(),
        P(),
        P(),
    )
    return jax.shard_map(
        body, mesh=mesh, in_specs=placed, out_specs=P("tile", "angle", None, None), check_vma=False
    )
```

profile of v0, /device:TPU:1, one launch (start us, length us, event | category | flops | bytes accessed | tf_op | source)
XLA Modules:
  0.0 744.5 jit_solution(15535922218430683627)
XLA Ops:
  11.3 3.1 copy.119
  14.4 14.0 %all-to-all-start = ((bf16[32,2,2,128,128]{4,3,2,1,0:T(8,128)(2,1)}), bf16[32,2,2,128,128]{4,3,2,1,0:T(8,128)(2,1)}, u32[]{:S(2)}, u32[]{:S(2)}) async-start(bf16[32,2,2,128,128]{4,3,2,1,0:T(8,128)(2,1)} %bitcast.193), calls=%async_computation | async-start | bytes 8388608 | tf_op jit(solution)/shard_map/all_to_all | solution.py:122
  29.0 91.9 %all-to-all-done = bf16[32,2,2,128,128]{4,3,2,1,0:T(8,128)(2,1)} async-done(((bf16[32,2,2,128,128]{4,3,2,1,0:T(8,128)(2,1)}), bf16[32,2,2,128,128]{4,3,2,1,0:T(8,128)(2,1)}, u32[]{:S(2)}, u32[]{:S(2)}) %all-to-all-start) | async-done | bytes 4194336 | tf_op jit(solution)/shard_map/all_to_all | solution.py:122
  121.0 2.7 fusion.82
  125.0 2.5 fusion.81
  127.5 4.1 copy.115
  131.6 2.9 copy.116
  134.5 2.9 pad_maximum_fusion
  141.9 6.8 fusion.35
  151.3 2.3 pad_maximum_fusion.1
  153.6 7.0 copy.112
  160.6 3.5 fusion.44
  164.1 2.3 copy.100
  166.4 9.7 %all-to-all-start.1 = ((bf16[32,2,2,128,128]{4,3,2,1,0:T(8,128)(2,1)}), bf16[32,2,2,128,128]{4,3,2,1,0:T(8,128)(2,1)}, u32[]{:S(2)}, u32[]{:S(2)}) async-start(bf16[32,2,2,128,128]{4,3,2,1,0:T(8,128)(2,1)} %copy.100), calls=%async_computation.1 | async-start | bytes 8388608 | tf_op jit(solution)/shard_map/all_to_all | solution.py:126
  176.2 92.5 %all-to-all-done.1 = bf16[32,2,2,128,128]{4,3,2,1,0:T(8,128)(2,1)} async-done(((bf16[32,2,2,128,128]{4,3,2,1,0:T(8,128)(2,1)}), bf16[32,2,2,128,128]{4,3,2,1,0:T(8,128)(2,1)}, u32[]{:S(2)}, u32[]{:S(2)}) %all-to-all-start.1) | async-done | bytes 4194336 | tf_op jit(solution)/shard_map/all_to_all | solution.py:126
  268.7 7.4 reshape.187
  276.1 2.9 convolution_convert_fusion.1
  279.6 60.2 %while.27 = (s32[]{:T(128)}, f32[512,1024]{1,0:T(8,128)S(1)}, s32[8]{0:T(128)S(1)}, s32[8]{0:T(128)S(1)}, f32[8,128,128]{2,1,0:T(8,128)S(1)}, /*index=5*/s32[]{:T(128)}, s32[]{:T(128)}, s32[]{:T(128)}, s32[]{:T(128)}) while((s32[]{:T(128)}, f32[512,1024]{1,0:T(8,128)S(1)}, s32[8]{0:T(128)S(1)}, s32[8]{0:T(128)S(1)}, ...), condition=%wide.region_3.4_spmd, body=%wide.region_2.3_spmd.sunk | while | flops 16392 | bytes 327881 | solution.py:143
  341.5 216.7 %reduce-scatter.2.cloned.1.call-done = bf16[16,1024]{1,0:T(8,128)(2,1)} async-done(((bf16[512,1024]{1,0:T(8,128)(2,1)}), bf16[16,1024]{1,0:T(8,128)(2,1)}) %reduce-scatter.2.cloned.1.call-update) | async-done | bytes 32784 | tf_op jit(solution)/shard_map/reduce_scatter | solution.py:144
  560.4 12.6 %all-to-all-start.2 = ((bf16[16,2,1024]{2,1,0:T(2,128)(2,1)}), bf16[16,2,1024]{2,1,0:T(2,128)(2,1)S(1)}, u32[]{:S(2)}, u32[]{:S(2)}) async-start(bf16[16,2,1024]{2,1,0:T(2,128)(2,1)} %multiply_convert_fusion), calls=%async_computation.3 | async-start | bytes 131072 | tf_op jit(solution)/shard_map/all_to_all | solution.py:157
  573.0 7.8 %all-to-all-done.2 = bf16[16,2,1024]{2,1,0:T(2,128)(2,1)S(1)} async-done(((bf16[16,2,1024]{2,1,0:T(2,128)(2,1)}), bf16[16,2,1024]{2,1,0:T(2,128)(2,1)S(1)}, u32[]{:S(2)}, u32[]{:S(2)}) %all-to-all-start.2) | async-done | bytes 65568 | tf_op jit(solution)/shard_map/all_to_all | solution.py:157
  580.9 46.0 %while.28 = (s32[]{:T(128)}, f32[2,16,1024]{2,1,0:T(8,128)S(1)}, f32[16,2,1024]{2,1,0:T(2,128)S(1)}, f32[16]{0:T(128)S(1)}, s32[]{:T(128)}, /*index=5*/s32[]{:T(128)}) while((s32[]{:T(128)}, f32[2,16,1024]{2,1,0:T(8,128)S(1)}, f32[16,2,1024]{2,1,0:T(2,128)S(1)}, f32[16]{0:T(128)S(1)}, s32[]{:T(128)}, ...), condition=%wide.region_7.8_spmd.clone.clone, body=%wide.region_6.7_spmd.clone.clone.sunk | while | flops 4391977 | bytes 844483 | solution.py:77
  628.7 8.3 %fusion.28 = bf16[16,2,8,129,16]{4,2,1,3,0:T(8,128)(2,1)S(1)} fusion(pred[16,129]{0,1:T(8,128)(4,1)S(1)} %copy-done.9, bf16[1,16,16,131]{2,0,3,1:T(2,128)(2,1)S(1)} %copy.106, bf16[16,1,3,3]{0,3,2,1:T(4,128)(2,1)S(1)} %copy-done), kind=kOutput, calls=%fused_computation.50 | convolution fusion | flops 11228160 | bytes 1126192 | tf_op jit(solution)/shard_map/conv_general_dilated | solution.py:84
  637.1 98.4 %fusion.25 = f32[16,16,129,1]{1,3,2,0:T(1,128)S(1)} fusion(bf16[16,2,7,1,16]{4,2,1,3,0:T(8,128)(2,1)S(1)} %get-tuple-element.258, bf16[16,2,7,1,16]{4,2,1,3,0:T(8,128)(2,1)S(1)} %get-tuple-element.257, bf16[16,2,8,129,16]{4,2,1,3,0:T(8,128)(2,1)S(1)} %fusion.28, bf16[1,16,3,3]{1,3,2,0:T(4,128)(2,1)S(1)} %copy-done.5), kind=kOutput, calls=%fused_computation.48 | convolution fusion | flops 14480384 | bytes 1203488 | tf_op jit(solution)/shard_map/conv_general_dilated | solution.py:88
  (436 shorter events, 92.3 us)
Async XLA Ops:
  6.5 622.2 %copy-start = (bf16[16,1,3,3]{0,3,2,1:T(4,128)(2,1)S(1)}, bf16[16,1,3,3]{0,3,2,1:T(4,128)(2,1)}, u32[]{:S(2)}) copy-start(bf16[16,1,3,3]{0,3,2,1:T(4,128)(2,1)} %param.22) | copy-start | bytes 868
  14.4 106.5 %all-to-all-start = ((bf16[32,2,2,128,128]{4,3,2,1,0:T(8,128)(2,1)}), bf16[32,2,2,128,128]{4,3,2,1,0:T(8,128)(2,1)}, u32[]{:S(2)}, u32[]{:S(2)}) async-start(bf16[32,2,2,128,128]{4,3,2,1,0:T(8,128)(2,1)} %bitcast.193), calls=%async_computation | async-start | bytes 8388608 | tf_op jit(solution)/shard_map/all_to_all | solution.py:122
  140.4 1.6 copy-start.2
  166.4 9.8 %copy-start.3 = (f32[2,128,128]{2,1,0:T(8,128)S(1)}, f32[2,128,128]{2,1,0:T(8,128)}, u32[]{:S(2)}) copy-start(f32[2,128,128]{2,1,0:T(8,128)} %param.16) | copy-start | bytes 393220
  166.4 102.4 %all-to-all-start.1 = ((bf16[32,2,2,128,128]{4,3,2,1,0:T(8,128)(2,1)}), bf16[32,2,2,128,128]{4,3,2,1,0:T(8,128)(2,1)}, u32[]{:S(2)}, u32[]{:S(2)}) async-start(bf16[32,2,2,128,128]{4,3,2,1,0:T(8,128)(2,1)} %copy.100), calls=%async_computation.1 | async-start | bytes 8388608 | tf_op jit(solution)/shard_map/all_to_all | solution.py:126
  176.1 382.1 %reduce-scatter.2.cloned.1.call-start = ((), (), s32[]{:S(2)}) async-start(), calls=%async_computation.4 | async-start | bytes 1081344 | tf_op jit(solution)/shard_map/reduce_scatter | solution.py:144
  276.1 3.5 copy-start.6
  276.1 3.5 copy-start.7
  279.3 61.7 %copy-start.4 = (s32[1,16]{1,0:T(1,128)S(1)}, s32[1,16]{1,0:T(1,128)}, u32[]{:S(2)}) copy-start(s32[1,16]{1,0:T(1,128)} %param.20) | copy-start | bytes 196
  279.6 301.3 %copy-start.8 = (f32[16]{0:T(128)S(1)}, f32[16]{0:T(128)}, u32[]{:S(2)}) copy-start(f32[16]{0:T(128)} %param.21) | copy-start | bytes 196
  559.6 69.1 %copy-start.9 = (pred[16,129]{0,1:T(8,128)(4,1)S(1)}, pred[16,129]{0,1:T(8,128)(4,1)}, u32[]{:S(2)}) copy-start(pred[16,129]{0,1:T(8,128)(4,1)} %constant.130) | copy-start | bytes 6196
  560.4 20.4 %all-to-all-start.2 = ((bf16[16,2,1024]{2,1,0:T(2,128)(2,1)}), bf16[16,2,1024]{2,1,0:T(2,128)(2,1)S(1)}, u32[]{:S(2)}, u32[]{:S(2)}) async-start(bf16[16,2,1024]{2,1,0:T(2,128)(2,1)} %multiply_convert_fusion), calls=%async_computation.3 | async-start | bytes 131072 | tf_op jit(solution)/shard_map/all_to_all | solution.py:157
  628.7 8.4 %copy-start.5 = (bf16[1,16,3,3]{1,3,2,0:T(4,128)(2,1)S(1)}, bf16[1,16,3,3]{1,3,2,0:T(4,128)(2,1)}, u32[]{:S(2)}) copy-start(bf16[1,16,3,3]{1,3,2,0:T(4,128)(2,1)} %param.23) | copy-start | bytes 868
  637.1 100.4 %copy-start.1 = (bf16[16,1,3,3]{0,3,2,1:T(4,128)(2,1)S(1)}, bf16[16,1,3,3]{0,3,2,1:T(4,128)(2,1)}, u32[]{:S(2)}) copy-start(bf16[16,1,3,3]{0,3,2,1:T(4,128)(2,1)} %param.22) | copy-start | bytes 868
Sparse Core Ops, SparseCore 0:
  341.1 217.0 reduce-scatter.1
where the time goes:
time: 749 us; the launch traced here: 745 us
  waiting for transfers between devices  409 us (55%)
  matrix products  123 us (16%)
  local copies, waits for them, and re-layouts  85.7 us (11%)
  other arithmetic  40.3 us (5%)
  starting transfers between devices  36.4 us (5%)
  loops' own time  35.7 us (5%)
  between operations  14 us (2%)
    reduce_scatter x1, waiting for transfers between devices, body(): lax.psum_scatter(canvas.astype(jnp.bfloat16), 'tile', scatter_dimension=0...  217 us
    conv_general_dilated x1, matrix products, prior(): lax.conv_general_dilated(hidden, prior_out.astype(jnp.float32), (1, 1), '...  98.4 us
    all_to_all x1, waiting for transfers between devices, body(): lax.all_to_all(fixed.reshape(tiles, depth, 2, side, side), 'tile', split_...  92.5 us
    all_to_all x1, waiting for transfers between devices, body(): lax.all_to_all(packed.reshape(tiles, depth, 2, side, side), 'tile', split...  91.9 us
    another operation x1, loops' own time, body(): canvas = lax.fori_loop(0, count, place, jnp.zeros((H, width), jnp.float32))  33.3 us
    dynamic_update_slice x8, local copies, waits for them, and re-layouts, place(): return lax.dynamic_update_slice(canvas, piece, (row, col))  15.5 us
  transfers between devices with their start and end apart: 4, of which 4 were waited for; matrix products, arithmetic and copies ran while one was open for 0% of the time, Pallas kernels for 0%

commit v1 on v0

v1 whole, which is shorter than its diff:
```python
import functools
import math

import jax
import jax.numpy as jnp
import numpy as np
from jax import lax
from jax.experimental import pallas as pl
from jax.experimental.pallas import tpu as pltpu
from jax.sharding import PartitionSpec as P

H = 512
W = 1024
XW = 16
CH = 16
SIDE = 128
COUNT = 8
TX = 4
TZ = 8
TILES = TX * TZ
ANGLES = 16
STRIP = H // TILES
SPREAD = 4
SHIFTS = 2 * SPREAD + 1
MESH = pl.DeviceIdType.MESH
BF = jnp.bfloat16
F32 = jnp.float32


def dft_table(side):
    index = np.arange(side)
    phase = ((index[:, None] * index[None, :]) % side).astype(np.float32)
    phase = phase * np.float32(2.0 * math.pi / side)
    scale = np.float32(1.0 / math.sqrt(side))
    real = np.cos(phase) * scale
    imag = -np.sin(phase) * scale
    upper = np.concatenate([real, imag], axis=1)
    lower = np.concatenate([-imag, real], axis=1)
    return np.concatenate([upper, lower], axis=0).astype(np.float32)


def exchange_kernel(owners, mags, out, recv, send_sem, recv_sem, own_sem):
    a = lax.axis_index("angle")
    me = lax.axis_index("tile")
    barrier = pltpu.get_barrier_semaphore()

    def greet(i, c):
        peer = lax.rem(me + i, TILES)
        pl.semaphore_signal(barrier, inc=1, device_id=(a, peer), device_id_type=MESH)
        return c

    lax.fori_loop(1, TILES, greet, 0)
    pl.semaphore_wait(barrier, TILES - 1)

    own = pltpu.make_async_copy(mags.at[pl.ds(me * 2, 2)], recv.at[pl.ds(me * 2, 2)], own_sem)
    own.start()

    def remote(i):
        peer = lax.rem(me + i, TILES)
        return pltpu.make_async_remote_copy(
            src_ref=mags.at[pl.ds(peer * 2, 2)],
            dst_ref=recv.at[pl.ds(me * 2, 2)],
            send_sem=send_sem.at[i],
            recv_sem=recv_sem.at[i],
            device_id=(a, peer),
            device_id_type=MESH,
        )

    def start(i, c):
        remote(i).start()
        return c

    lax.fori_loop(1, TILES, start, 0)

    def finish(i, c):
        source = lax.rem(me - i + TILES, TILES)
        copy = pltpu.make_async_remote_copy(
            src_ref=mags.at[pl.ds(source * 2, 2)],
            dst_ref=recv.at[pl.ds(source * 2, 2)],
            send_sem=send_sem.at[i],
            recv_sem=recv_sem.at[i],
            device_id=(a, source),
            device_id_type=MESH,
        )
        copy.wait_recv()
        copy.wait_send()
        return c

    lax.fori_loop(1, TILES, finish, 0)
    own.wait()

    ids = [owners[0, k] for k in range(COUNT)]
    for k in range(COUNT):
        rank = jnp.int32(0)
        for j in range(k):
            rank = rank + jnp.where(ids[j] == ids[k], 1, 0).astype(jnp.int32)
        out[k] = recv[ids[k] * 2 + rank]


def canvas_kernel(rows, cols, patches, level, probe, table, table_t, out, canvas):
    canvas[...] = jnp.zeros_like(canvas)
    pair = 2
    for g in range(COUNT // pair):
        ks = [g * pair + j for j in range(pair)]
        joined = jnp.concatenate(
            [jnp.concatenate([patches[k, 0], patches[k, 1]], axis=1) for k in ks], axis=0
        )
        half = jnp.dot(joined, table[...], preferred_element_type=F32).astype(BF)
        stacked = jnp.concatenate(
            [
                jnp.concatenate([half[j * SIDE : (j + 1) * SIDE, q * SIDE : (q + 1) * SIDE] for j in range(pair)], axis=1)
                for q in range(2)
            ],
            axis=0,
        )
        spectrum = jnp.dot(table_t[...], stacked, preferred_element_type=F32)
        real = spectrum[:SIDE]
        imag = spectrum[SIDE:]
        measured = jnp.concatenate([level[k] for k in ks], axis=1).astype(F32)
        factor = measured * lax.rsqrt(real * real + imag * imag + 0.25)
        real = (real * factor).astype(BF)
        imag = (imag * factor).astype(BF)
        target = jnp.concatenate(
            [
                jnp.concatenate([real[:, j * SIDE : (j + 1) * SIDE], imag[:, j * SIDE : (j + 1) * SIDE]], axis=1)
                for j in range(pair)
            ],
            axis=0,
        )
        back = jnp.dot(target, table_t[...], preferred_element_type=F32).astype(BF)
        stacked = jnp.concatenate(
            [
                jnp.concatenate([back[j * SIDE : (j + 1) * SIDE, q * SIDE : (q + 1) * SIDE] for j in range(pair)], axis=1)
                for q in range(2)
            ],
            axis=0,
        )
        result = jnp.dot(table[...], stacked, preferred_element_type=F32)
        for j in range(pair):
            k = ks[j]
            part = slice(j * SIDE, (j + 1) * SIDE)
            contrib = (probe[0] * result[SIDE:, part] - probe[1] * result[:SIDE, part]) * 0.25
            row = rows[0, k]
            col = cols[0, k]
            low_row = row // 8
            low_col = col // SIDE
            wide = jnp.concatenate([contrib, jnp.zeros((SIDE, SIDE), F32)], axis=1)
            wide = pltpu.roll(wide, col - low_col * SIDE, 1)
            tall = jnp.concatenate([wide, jnp.zeros((8, 2 * SIDE), F32)], axis=0)
            tall = pltpu.roll(tall, row - low_row * 8, 0)
            at = (pl.ds(pl.multiple_of(low_row * 8, 8), SIDE + 8), pl.ds(pl.multiple_of(low_col * SIDE, SIDE), 2 * SIDE))
            canvas[at] = canvas[at] + tall
    out[...] = canvas[:H, :W].astype(BF)


def strip_kernel(
    lengths, canvas, out, mine, from_x, part, from_z, sel, pieces, sino, own_sem, xs, xr, zs, zr, as_, ar
):
    a = lax.axis_index("angle")
    me = lax.axis_index("tile")
    x = me // TZ
    z = lax.rem(me, TZ)
    barrier = pltpu.get_barrier_semaphore()
    rows = TZ * STRIP

    def at_x(i):
        return lax.rem(x + i, TX) * TZ + z

    def at_z(i):
        return x * TZ + lax.rem(z + i, TZ)

    def greet(which, axis_angle):
        def run(i, c):
            if axis_angle:
                target = (lax.rem(a + i, ANGLES), me)
            else:
                target = (a, which(i))
            pl.semaphore_signal(barrier, inc=1, device_id=target, device_id_type=MESH)
            return c

        return run

    lax.fori_loop(1, TX, greet(at_x, False), 0)
    lax.fori_loop(1, TZ, greet(at_z, False), 0)
    lax.fori_loop(1, ANGLES, greet(None, True), 0)
    pl.semaphore_wait(barrier, TX + TZ + ANGLES - 3)

    own = pltpu.make_async_copy(canvas.at[pl.ds(x * rows, rows)], mine, own_sem)
    own.start()

    def copy_x(i):
        peer = at_x(i)
        return pltpu.make_async_remote_copy(
            src_ref=canvas.at[pl.ds((peer // TZ) * rows, rows)],
            dst_ref=from_x.at[i],
            send_sem=xs.at[i],
            recv_sem=xr.at[i],
            device_id=(a, peer),
            device_id_type=MESH,
        )

    for i in (2, 1, 3):
        copy_x(i).start()

    row_id = lax.broadcasted_iota(jnp.int32, (16, 128), 0)
    lane_id = lax.broadcasted_iota(jnp.int32, (16, 128), 1)
    within = row_id % 2
    same = (row_id // 2) == (lane_id // 16)
    place = lane_id % 16 - within
    begin = jnp.int32(0)
    for b in range(ANGLES):
        length = lengths[0, b]
        hit = same & (place == begin) & (within < length)
        sel[b] = hit.astype(F32).astype(BF)
        begin = begin + length

    own.wait()
    for i in (1, 3, 2):
        copy_x(i).wait_recv()
    total = mine[...].astype(F32)
    for i in range(1, TX):
        total = total + from_x[i].astype(F32)
    total = total.astype(BF)
    for j in range(TZ):
        part[j] = total[j * STRIP : (j + 1) * STRIP]

    def copy_z(i):
        peer = at_z(i)
        return pltpu.make_async_remote_copy(
            src_ref=part.at[lax.rem(peer, TZ)],
            dst_ref=from_z.at[i],
            send_sem=zs.at[i],
            recv_sem=zr.at[i],
            device_id=(a, peer),
            device_id_type=MESH,
        )

    for i in (4, 3, 5, 2, 6, 1, 7):
        copy_z(i).start()
    strip = part[z].astype(F32)
    for i in (1, 7, 2, 6, 3, 5, 4):
        copy_z(i).wait_recv()
        strip = strip + from_z[i].astype(F32)
    strip = strip.astype(BF)
    blocks = jnp.concatenate([strip[:, c * 128 : (c + 1) * 128] for c in range(W // 128)], axis=0)
    chosen = jnp.dot(sel[...].reshape(ANGLES * 16, 128), blocks, preferred_element_type=F32)
    pieces[...] = chosen.astype(BF).reshape(ANGLES, 16, 128)

    def copy_a(i):
        peer = lax.rem(a + i, ANGLES)
        return pltpu.make_async_remote_copy(
            src_ref=pieces.at[peer],
            dst_ref=sino.at[a],
            send_sem=as_.at[i],
            recv_sem=ar.at[i],
            device_id=(peer, me),
            device_id_type=MESH,
        )

    def start_a(i, c):
        copy_a(i).start()
        return c

    lax.fori_loop(1, ANGLES, start_a, 0)
    sino[a] = pieces[a]

    def finish_a(i, c):
        source = lax.rem(a - i + ANGLES, ANGLES)
        pltpu.make_async_remote_copy(
            src_ref=pieces.at[source],
            dst_ref=sino.at[source],
            send_sem=as_.at[i],
            recv_sem=ar.at[i],
            device_id=(source, me),
            device_id_type=MESH,
        ).wait_recv()
        return c

    lax.fori_loop(1, ANGLES, finish_a, 0)
    out[...] = sino[...]
    for i in range(1, TX):
        copy_x(i).wait_send()
    for i in range(1, TZ):
        copy_z(i).wait_send()

    def sent_a(i, c):
        copy_a(i).wait_send()
        return c

    lax.fori_loop(1, ANGLES, sent_a, 0)


def shifted(values, step):
    if step == 0:
        return values
    lane = lax.broadcasted_iota(jnp.int32, values.shape, 1) + step
    rolled = pltpu.roll(values, (-step) % W, 1)
    return jnp.where((lane >= 0) & (lane < W), rolled, 0.0)


def slab_kernel(first, second, tangents, sino, out, flat, k_in, k_out):
    rows = SHIFTS * XW
    row = lax.broadcasted_iota(jnp.int32, (rows, ANGLES), 0)
    offset = (row % XW).astype(F32) - (XW - 1) / 2.0
    shift = (row // XW).astype(F32) - float(SPREAD)
    weight = jnp.maximum(1.0 - jnp.abs(offset * tangents[...] - shift), 0.0) * (1.0 / ANGLES)
    high = weight.astype(BF)
    low = (weight - high.astype(F32)).astype(BF)
    weights = jnp.concatenate([high, low], axis=1)

    r16 = lax.broadcasted_iota(jnp.int32, (XW, 128), 0)
    lane = lax.broadcasted_iota(jnp.int32, (XW, 128), 1)
    masks = [
        [((lane // XW == dj) & (lane % XW == r16 + di - 1)).astype(F32) for dj in range(3)] for di in range(3)
    ]
    for ch in range(CH):
        total = jnp.zeros((XW, 128), F32)
        for di in range(3):
            for dj in range(3):
                total = total + masks[di][dj] * first[ch, di * 3 + dj]
        k_in[ch * XW : (ch + 1) * XW, :] = total.astype(BF)
    near = [(lane % XW == r16 + di - 1) for di in range(3)]
    marks = [[(near[di] & (lane // XW == q)).astype(F32) for di in range(3)] for q in range(8)]
    for block in range(CH // 8):
        for dj in range(3):
            total = jnp.zeros((XW, 128), F32)
            for q in range(8):
                for di in range(3):
                    total = total + marks[q][di] * second[block * 8 + q, di * 3 + dj]
            k_out[dj * XW : (dj + 1) * XW, block * 128 : (block + 1) * 128] = total.astype(BF)

    flat[...] = sino[...].astype(F32).reshape(ANGLES * 16, 128)
    for r in range(2):
        rows_r = jnp.concatenate(
            [flat[pl.ds(2 * c + r, ANGLES, stride=16), :] for c in range(W // 128)], axis=1
        ).astype(BF)
        both = jnp.concatenate([rows_r, rows_r], axis=0)
        spread = jnp.dot(weights, both, preferred_element_type=F32)
        picture = jnp.zeros((XW, W), F32)
        for s in range(SHIFTS):
            picture = picture + shifted(spread[s * XW : (s + 1) * XW], s - SPREAD)
        rounded = picture.astype(BF).astype(F32)
        stack = jnp.concatenate([shifted(rounded, dj - 1) for dj in range(3)], axis=0).astype(BF)
        hidden = jnp.dot(k_in[:, : 3 * XW], stack, preferred_element_type=F32)
        hidden = jnp.maximum(hidden, 0.0).astype(BF)
        extra = jnp.dot(k_out[...], hidden, preferred_element_type=F32)
        for dj in range(3):
            picture = picture + shifted(extra[dj * XW : (dj + 1) * XW], dj - 1)
        out[r] = picture


def body(patches, magnitudes, probe, owners, scan_rows, scan_cols, slab_rows, angle_tan, prior_in, prior_out):
    vmem = pl.BlockSpec(memory_space=pltpu.VMEM)
    smem = pl.BlockSpec(memory_space=pltpu.SMEM)
    hbm = pl.BlockSpec(memory_space=pl.ANY)
    dma = pltpu.SemaphoreType.DMA
    limit = 48 * 1024 * 1024
    numbers = dft_table(SIDE)
    table = jnp.asarray(numbers).astype(BF)
    table_t = jnp.asarray(np.ascontiguousarray(numbers.T)).astype(BF)

    level = pl.pallas_call(
        exchange_kernel,
        out_shape=jax.ShapeDtypeStruct((COUNT, SIDE, SIDE), BF),
        in_specs=[smem, hbm],
        out_specs=vmem,
        scratch_shapes=[
            pltpu.VMEM((2 * TILES, SIDE, SIDE), BF),
            dma((TILES,)),
            dma((TILES,)),
            dma,
        ],
        compiler_params=pltpu.CompilerParams(collective_id=0, has_side_effects=True, vmem_limit_bytes=limit),
        name="frames",
    )(owners.reshape(1, COUNT), magnitudes[0])

    canvas = pl.pallas_call(
        canvas_kernel,
        out_shape=jax.ShapeDtypeStruct((H, W), BF),
        in_specs=[smem, smem, vmem, vmem, vmem, vmem, vmem],
        out_specs=vmem,
        scratch_shapes=[pltpu.VMEM((H + 8, W + SIDE), F32)],
        compiler_params=pltpu.CompilerParams(vmem_limit_bytes=limit),
        name="canvas",
    )(scan_rows, scan_cols, patches[0], level, probe, table, table_t)

    rows = TZ * STRIP
    sino = pl.pallas_call(
        strip_kernel,
        out_shape=jax.ShapeDtypeStruct((ANGLES, 16, 128), BF),
        in_specs=[smem, hbm],
        out_specs=vmem,
        scratch_shapes=[
            pltpu.VMEM((rows, W), BF),
            pltpu.VMEM((TX, rows, W), BF),
            pltpu.VMEM((TZ, STRIP, W), BF),
            pltpu.VMEM((TZ, STRIP, W), BF),
            pltpu.VMEM((ANGLES, 16, 128), BF),
            pltpu.VMEM((ANGLES, 16, 128), BF),
            pltpu.VMEM((ANGLES, 16, 128), BF),
            dma,
            dma((TX,)),
            dma((TX,)),
            dma((TZ,)),
            dma((TZ,)),
            dma((ANGLES,)),
            dma((ANGLES,)),
        ],
        compiler_params=pltpu.CompilerParams(collective_id=1, has_side_effects=True, vmem_limit_bytes=limit),
        name="strips",
    )(slab_rows, canvas)

    volume = pl.pallas_call(
        slab_kernel,
        out_shape=jax.ShapeDtypeStruct((2, XW, W), F32),
        in_specs=[smem, smem, vmem, vmem],
        out_specs=vmem,
        scratch_shapes=[
            pltpu.VMEM((ANGLES * 16, 128), F32),
            pltpu.VMEM((CH * XW, 128), BF),
            pltpu.VMEM((3 * XW, CH * XW), BF),
        ],
        compiler_params=pltpu.CompilerParams(vmem_limit_bytes=limit),
        name="slabs",
    )(
        prior_in.astype(F32).reshape(CH, 9),
        prior_out.astype(F32).reshape(CH, 9),
        angle_tan.reshape(1, ANGLES),
        sino,
    )
    return volume[None]


def solution(mesh):
    placed = (
        P("angle", "tile", None, None, None),
        P("angle", "tile", None, None),
        P(),
        P("angle", "tile", None),
        P("angle", "tile"),
        P("angle", "tile"),
        P("tile", None),
        P(),
        P(),
        P(),
    )
    return jax.shard_map(
        body, mesh=mesh, in_specs=placed, out_specs=P("tile", "angle", None, None), check_vma=False
    )
```

time: 749 us -> 106 us (0.14)
  waiting for transfers between devices: 409 us -> 0 us
  matrix products: 123 us -> 0 us
  Pallas kernels: 0 us -> 103 us
  local copies, waits for them, and re-layouts: 85.7 us -> 2.5 us
  other arithmetic: 40.3 us -> 0 us
  starting transfers between devices: 36.4 us -> 0 us
  loops' own time: 35.7 us -> 0 us
  between operations: 14 us -> 0.14 us
    reduce_scatter x1 -> x0, waiting for transfers between devices: 217 us -> none  [body(): lax.psum_scatter(canvas.astype(jnp.bfloat16), 'tile', scatter_dimension=0...]
    all_to_all x3 -> x0, waiting for transfers between devices: 192 us -> none  [the longest x1 92.5 us: body(): lax.all_to_all(fixed.reshape(tiles, depth, 2, side, side), 'tile', split_...]
    conv_general_dilated x2 -> x0, matrix products: 107 us -> none  [the longest x1 98.4 us: prior(): lax.conv_general_dilated(hidden, prior_out.astype(jnp.float32), (1, 1), '...]
    pallas_call x0 -> x4, Pallas kernels: none -> 103 us  [the longest x1 59.6 us: body(): pl.pallas_call(exchange_kernel, out_shape=jax.ShapeDtypeStruct((COUNT, SI...]
    all_to_all x3 -> x0, starting transfers between devices: 36.4 us -> none  [the longest x1 14 us: body(): lax.all_to_all(packed.reshape(tiles, depth, 2, side, side), 'tile', split...]
    another operation x2 -> x0, loops' own time: 35.7 us -> none  [the longest x1 33.3 us: body(): canvas = lax.fori_loop(0, count, place, jnp.zeros((H, width), jnp.float32))]
    dynamic_slice x64 -> x0, local copies, waits for them, and re-layouts: 20.4 us -> none  [the longest x48 9.74 us: backproject(): total, unused = lax.scan(add_angle, start, (sino, angle_tan))]
    dot_general x22 -> x0, matrix products: 16.6 us -> none  [the longest x16 5.17 us: add_angle(): jnp.einsum('is,scj->cij', weights, columns_stack, precision=lax.Precision...]
  transfers between devices with their start and end apart: 4 -> 0, of which waited for: 4 -> 0; matrix products, arithmetic and copies ran while one was open for 0% -> 0% of each run, Pallas kernels for 0% -> 0%
where the time goes in v1:
time: 106 us; the launch traced here: 105 us
  Pallas kernels  103 us (97%)
  local copies, waits for them, and re-layouts  2.5 us (2%)
    pallas_call x1, Pallas kernels, body(): pl.pallas_call(exchange_kernel, out_shape=jax.ShapeDtypeStruct((COUNT, SI...  59.6 us
    pallas_call x1, Pallas kernels, body(): pl.pallas_call(strip_kernel, out_shape=jax.ShapeDtypeStruct((ANGLES, 16,...  36.9 us
    pallas_call x1, Pallas kernels, body(): pl.pallas_call(canvas_kernel, out_shape=jax.ShapeDtypeStruct((H, W), BF),...  3.16 us
    pallas_call x1, Pallas kernels, body(): pl.pallas_call(slab_kernel, out_shape=jax.ShapeDtypeStruct((2, XW, W), F3...  3.13 us
    unnamed x24, local copies, waits for them, and re-layouts  2.32 us

profile of v1, /device:TPU:1, one launch (start us, length us, event | category | flops | bytes accessed | tf_op | source)
XLA Modules:
  0.0 105.5 jit_solution(11054049691932243300)
XLA Ops:
  0.0 0.0 copy-start.8
  0.0 0.0 copy-start.9
  0.0 1.6 %copy-done = bf16[1,64,128,128]{3,2,1,0:T(8,128)(2,1)S(1)} copy-done((bf16[1,64,128,128]{3,2,1,0:T(8,128)(2,1)S(1)}, bf16[1,64,128,128]{3,2,1,0:T(8,128)(2,1)}, u32[]{:S(2)}) %copy-start) | copy-done | bytes 2097176
  1.6 0.7 copy-done.5
  2.3 0.0 copy-start.6
  2.3 59.6 %frames.1.level = bf16[8,128,128]{2,1,0:T(8,128)(2,1)S(1)} custom-call(s32[1,8]{1,0:T(1,128)S(1)} %bitcast.11, bf16[64,128,128]{2,1,0:T(8,128)(2,1)S(1)} %bitcast.9), custom_call_target="tpu_custom_call" | custom-call | tf_op jit(solution)/shard_map/frames/pallas_call | solution.py:362
  61.9 0.0 copy-start.10
  61.9 0.0 copy-start.11
  61.9 0.0 copy-start.7
  62.0 0.0 copy-done.8
  62.0 0.0 copy-done.9
  62.0 0.0 copy-done.1
  62.0 0.0 copy-done.2
  62.0 0.0 copy-done.3
  62.0 0.0 copy-done.4
  62.0 3.2 %canvas.1 = bf16[512,1024]{1,0:T(8,128)(2,1)S(1)} custom-call(s32[1,8]{1,0:T(1,128)S(1)} %copy-done.8, s32[1,8]{1,0:T(1,128)S(1)} %copy-done.9, bf16[8,2,128,128]{3,2,1,0:T(8,128)(2,1)S(1)} %bitcast.10, bf16[8,128,128]{2,1,0:T(8,128)(2,1)S(1)} %frames.1.level, f32[2,128,128]{2,1,0:T(8,128)S(1)} %copy-done.2, bf16[256,256]{1,0:T(8,128)(2,1)S(1)} %copy-done.3, ...), custom_call_target="tpu_custom_call" | custom-call | tf_op jit(solution)/shard_map/canvas/pallas_call | solution.py:377
  65.2 0.0 copy-done.6
  65.2 36.9 %strips.1.sino = bf16[16,16,128]{2,1,0:T(8,128)(2,1)S(1)} custom-call(s32[1,16]{1,0:T(1,128)S(1)} %copy-done.6, bf16[512,1024]{1,0:T(8,128)(2,1)S(1)} %canvas.1), custom_call_target="tpu_custom_call" | custom-call | tf_op jit(solution)/shard_map/strips/pallas_call | solution.py:388
  102.1 0.0 copy-done.10
  102.2 0.1 copy.15.first
  102.3 0.0 copy-done.11
  102.3 0.1 copy.16.second
  102.4 0.0 copy-done.7
  102.4 3.1 %slabs.1 = f32[2,16,1024]{2,1,0:T(8,128)} custom-call(f32[16,9]{1,0:T(8,128)S(1)} %copy.15.first, f32[16,9]{1,0:T(8,128)S(1)} %copy.16.second, f32[1,16]{1,0:T(1,128)S(1)} %bitcast.12, bf16[16,16,128]{2,1,0:T(8,128)(2,1)S(1)} %strips.1.sino), custom_call_target="tpu_custom_call" | custom-call | tf_op jit(solution)/shard_map/slabs/pallas_call | solution.py:413
  (8 shorter events, 0.0 us)
Async XLA Ops:
  0.0 62.0 %copy-start.8 = (s32[1,8]{1,0:T(1,128)S(1)}, s32[1,8]{1,0:T(1,128)}, u32[]{:S(2)}) copy-start(s32[1,8]{1,0:T(1,128)} %rows.1) | copy-start | bytes 100
  0.0 62.0 %copy-start.9 = (s32[1,8]{1,0:T(1,128)S(1)}, s32[1,8]{1,0:T(1,128)}, u32[]{:S(2)}) copy-start(s32[1,8]{1,0:T(1,128)} %cols.1) | copy-start | bytes 100
  0.0 1.6 %copy-start = (bf16[1,64,128,128]{3,2,1,0:T(8,128)(2,1)S(1)}, bf16[1,64,128,128]{3,2,1,0:T(8,128)(2,1)}, u32[]{:S(2)}) copy-start(bf16[1,64,128,128]{3,2,1,0:T(8,128)(2,1)} %param.13) | copy-start | bytes 6291460
  1.6 0.7 copy-start.5
  2.3 59.7 %copy-start.1 = (bf16[1,8,2,128,128]{4,3,2,1,0:T(8,128)(2,1)S(1)}, bf16[1,8,2,128,128]{4,3,2,1,0:T(8,128)(2,1)}, u32[]{:S(2)}) copy-start(bf16[1,8,2,128,128]{4,3,2,1,0:T(8,128)(2,1)} %param.12) | copy-start | bytes 1572868
  2.3 59.7 %copy-start.2 = (f32[2,128,128]{2,1,0:T(8,128)S(1)}, f32[2,128,128]{2,1,0:T(8,128)}, u32[]{:S(2)}) copy-start(f32[2,128,128]{2,1,0:T(8,128)} %probe.1) | copy-start | bytes 393220
  2.3 59.7 %copy-start.3 = (bf16[256,256]{1,0:T(8,128)(2,1)S(1)}, bf16[256,256]{1,0:T(8,128)(2,1)}, u32[]{:S(2)}) copy-start(bf16[256,256]{1,0:T(8,128)(2,1)} %constant.12.table) | copy-start | bytes 393220
  2.3 59.7 %copy-start.4 = (bf16[256,256]{1,0:T(8,128)(2,1)S(1)}, bf16[256,256]{1,0:T(8,128)(2,1)}, u32[]{:S(2)}) copy-start(bf16[256,256]{1,0:T(8,128)(2,1)} %constant.13.table_t) | copy-start | bytes 393220
  2.3 62.9 %copy-start.6 = (s32[1,16]{1,0:T(1,128)S(1)}, s32[1,16]{1,0:T(1,128)}, u32[]{:S(2)}) copy-start(s32[1,16]{1,0:T(1,128)} %lengths.1) | copy-start | bytes 196
  61.9 40.2 %copy-start.10 = (bf16[16,1,3,3]{0,3,2,1:T(4,128)(2,1)S(1)}, bf16[16,1,3,3]{0,3,2,1:T(4,128)(2,1)}, u32[]{:S(2)}) copy-start(bf16[16,1,3,3]{0,3,2,1:T(4,128)(2,1)} %param.20) | copy-start | bytes 868
  61.9 40.3 %copy-start.11 = (bf16[1,16,3,3]{1,3,2,0:T(4,128)(2,1)S(1)}, bf16[1,16,3,3]{1,3,2,0:T(4,128)(2,1)}, u32[]{:S(2)}) copy-start(bf16[1,16,3,3]{1,3,2,0:T(4,128)(2,1)} %param.21) | copy-start | bytes 868
  61.9 40.4 %copy-start.7 = (f32[16]{0:T(128)S(1)}, f32[16]{0:T(128)}, u32[]{:S(2)}) copy-start(f32[16]{0:T(128)} %param.19) | copy-start | bytes 196

commit v2 on v1

v2 whole, which is shorter than its diff:
```python
import math

import jax
import jax.numpy as jnp
import numpy as np
from jax import lax
from jax.experimental import pallas as pl
from jax.experimental.pallas import tpu as pltpu
from jax.sharding import PartitionSpec as P

H = 512
W = 1024
XW = 16
CH = 16
SIDE = 128
COUNT = 8
TX = 4
TZ = 8
TILES = TX * TZ
ANGLES = 16
STRIP = H // TILES
SPREAD = 4
SHIFTS = 2 * SPREAD + 1
HALF = COUNT // 2
CHUNKS = 4
WIDE = W // CHUNKS
AHEAD = 3
ORDER = (4, 3, -3, 2, -2, 1, -1, 0)
CHAINS = ((1, 4, 0), (-1, 3, 0), (1, 3, HALF), (-1, 4, HALF))
MESH = pl.DeviceIdType.MESH
BF = jnp.bfloat16
F32 = jnp.float32


def dft_table(side):
    index = np.arange(side)
    phase = ((index[:, None] * index[None, :]) % side).astype(np.float32)
    phase = phase * np.float32(2.0 * math.pi / side)
    scale = np.float32(1.0 / math.sqrt(side))
    real = np.cos(phase) * scale
    imag = -np.sin(phase) * scale
    upper = np.concatenate([real, imag], axis=1)
    lower = np.concatenate([-imag, real], axis=1)
    return np.concatenate([upper, lower], axis=0).astype(np.float32)


def fused_kernel(
    owners, rows, cols, lengths, patches, mags, probe, table, table_t, out,
    f0, f1, f2, f3, f4, f5, f6, f7, c0, c1, c2, c3,
    waves, light, fwd, fwd_t, ids_out, ids_in, ids_s, spec, hot, placed, stage, from_x, mine, part, from_z, sel,
    pieces, sino, loc, xs, xr, cs, cr, is_, ir, ls, sxs, sxr, szs, szr, as_, ar,
):
    frames = (f0, f1, f2, f3, f4, f5, f6, f7)
    chains = (c0, c1, c2, c3)
    a = lax.axis_index("angle")
    me = lax.axis_index("tile")
    x = me // TZ
    z = lax.rem(me, TZ)
    rows_x = TZ * STRIP

    def at_x(i):
        return lax.rem(x + i, TX) * TZ + z

    def at_z(i):
        return x * TZ + lax.rem(z + i + TZ, TZ)

    local = [
        pltpu.make_async_copy(patches, waves, loc.at[8]),
        pltpu.make_async_copy(table, fwd, loc.at[9]),
        pltpu.make_async_copy(table_t, fwd_t, loc.at[10]),
        pltpu.make_async_copy(probe, light, loc.at[11]),
    ]
    for copy in local:
        copy.start()

    def source_z(d):
        return lax.rem(z + d + TZ, TZ)

    def own_frames(q):
        return pltpu.make_async_copy(
            mags.at[pl.ds((x * TZ + source_z(ORDER[q])) * 2, 2)], frames[q].at[pl.ds(x * 2, 2)], loc.at[q]
        )

    for q in range(TZ):
        own_frames(q).start()

    barrier = pltpu.get_barrier_semaphore()
    for i in range(1, TX):
        pl.semaphore_signal(barrier, inc=1, device_id=(a, at_x(i)), device_id_type=MESH)
    for i in range(1, TZ):
        pl.semaphore_signal(barrier, inc=1, device_id=(a, at_z(i)), device_id_type=MESH)

    def greet(i, c):
        pl.semaphore_signal(barrier, inc=1, device_id=(lax.rem(a + i, ANGLES), me), device_id_type=MESH)
        return c

    lax.fori_loop(1, ANGLES, greet, 0)

    mine_ids = [owners[0, k] for k in range(COUNT)]
    lane = lax.broadcasted_iota(jnp.int32, (8, 128), 1)
    vector = jnp.zeros((8, 128), jnp.int32)
    for k in range(COUNT):
        vector = jnp.where(lane == k, mine_ids[k], vector)
    ids_out[...] = vector
    pl.semaphore_wait(barrier, TX + TZ + ANGLES - 3)

    def copy_ids(i):
        return pltpu.make_async_remote_copy(
            src_ref=ids_out, dst_ref=ids_in.at[i], send_sem=is_.at[i], recv_sem=ir.at[i],
            device_id=(a, at_z(i)), device_id_type=MESH,
        )

    for i in (4, 3, 5, 2, 6, 1, 7):
        copy_ids(i).start()

    def copy_x(q, i):
        peer = at_x(i)
        return pltpu.make_async_remote_copy(
            src_ref=mags.at[pl.ds(((peer // TZ) * TZ + source_z(ORDER[q])) * 2, 2)],
            dst_ref=frames[q].at[pl.ds(x * 2, 2)],
            send_sem=xs.at[q, i], recv_sem=xr.at[q, i],
            device_id=(a, peer), device_id_type=MESH,
        )

    def start_x(q):
        for i in (2, 1, 3):
            copy_x(q, i).start()

    for q in range(AHEAD):
        start_x(q)

    row_id = lax.broadcasted_iota(jnp.int32, (16, 128), 0)
    lane_id = lax.broadcasted_iota(jnp.int32, (16, 128), 1)
    within = row_id % 2
    same = (row_id // 2) == (lane_id // 16)
    place = lane_id % 16 - within
    begin = jnp.int32(0)
    for b in range(ANGLES):
        length = lengths[0, b]
        hit = same & (place == begin) & (within < length)
        sel[b] = hit.astype(F32).astype(BF)
        begin = begin + length
    gap = lax.broadcasted_iota(jnp.int32, (H, 128), 0) - lax.broadcasted_iota(jnp.int32, (H, 128), 1)
    for k in range(COUNT):
        hot[:, k * SIDE : (k + 1) * SIDE] = (gap == rows[0, k]).astype(F32).astype(BF)

    pair = 2

    def stack(values):
        return jnp.concatenate(
            [
                jnp.concatenate(
                    [values[j * SIDE : (j + 1) * SIDE, p * SIDE : (p + 1) * SIDE] for j in range(pair)], axis=1
                )
                for p in range(2)
            ],
            axis=0,
        )

    for copy in local:
        copy.wait()
    for g in range(COUNT // pair):
        joined = jnp.concatenate(
            [jnp.concatenate([waves[k, 0], waves[k, 1]], axis=1) for k in range(g * pair, (g + 1) * pair)], axis=0
        )
        half = jnp.dot(joined, fwd[...], preferred_element_type=F32).astype(BF)
        spec[:, g * pair * SIDE : (g + 1) * pair * SIDE] = jnp.dot(
            fwd_t[...], stack(half), preferred_element_type=F32
        )

    for i in (1, 7, 2, 6, 3, 5, 4):
        copy_ids(i).wait_recv()
    to_scalar = pltpu.make_async_copy(ids_in, ids_s, ls)
    to_scalar.start()
    to_scalar.wait()

    def chosen(q):
        d = ORDER[q]
        ids = mine_ids if d == 0 else [ids_s[(-d) % TZ, 0, k] for k in range(COUNT)]

        def one(k):
            rank = jnp.int32(0)
            for j in range(k):
                rank = rank + jnp.where(ids[j] == ids[k], 1, 0).astype(jnp.int32)
            return (ids[k] & 7) == z, frames[q][((ids[k] >> 3) & 3) * 2 + (rank & 1)]

        return one

    def copy_chain(c, level):
        step = CHAINS[c][0]
        return pltpu.make_async_remote_copy(
            src_ref=chains[c].at[level], dst_ref=chains[c].at[level - 1],
            send_sem=cs.at[c, level], recv_sem=cr.at[c, level - 1],
            device_id=(a, at_z(step)), device_id_type=MESH,
        )

    for q in range(TZ):
        if q + AHEAD < TZ:
            start_x(q + AHEAD)
        own_frames(q).wait()
        for i in (1, 3, 2):
            copy_x(q, i).wait_recv()
        pick = chosen(q)
        d = ORDER[q]
        if d == 0:
            for c in range(4):
                copy_chain(c, 1).wait_recv()
            break
        for c in range(4):
            step, first, base = CHAINS[c]
            level = 4 if d == 4 else step * d
            if level < 1 or level > first:
                continue
            if level < first:
                copy_chain(c, level + 1).wait_recv()
            for k in range(HALF):
                hit, frame = pick(base + k)
                before = chains[c][level, k] if level < first else jnp.zeros((SIDE, SIDE), BF)
                chains[c][level, k] = jnp.where(hit, frame, before)
            copy_chain(c, level).start()

    for g in range(COUNT // pair):
        ks = [g * pair + j for j in range(pair)]
        measured = []
        for k in ks:
            hit, frame = pick(k)
            two = (0, 1) if k < HALF else (2, 3)
            came = chains[two[0]][0, k % HALF] + chains[two[1]][0, k % HALF]
            measured.append(jnp.where(hit, frame, came).astype(F32))
        part_g = slice(g * pair * SIDE, (g + 1) * pair * SIDE)
        real = spec[:SIDE, part_g]
        imag = spec[SIDE:, part_g]
        factor = jnp.concatenate(measured, axis=1) * lax.rsqrt(real * real + imag * imag + 0.25)
        real = (real * factor).astype(BF)
        imag = (imag * factor).astype(BF)
        target = jnp.concatenate(
            [
                jnp.concatenate([real[:, j * SIDE : (j + 1) * SIDE], imag[:, j * SIDE : (j + 1) * SIDE]], axis=1)
                for j in range(pair)
            ],
            axis=0,
        )
        back = jnp.dot(target, fwd_t[...], preferred_element_type=F32).astype(BF)
        result = jnp.dot(fwd[...], stack(back), preferred_element_type=F32)
        for j in range(pair):
            k = ks[j]
            at = slice(j * SIDE, (j + 1) * SIDE)
            contrib = (light[0] * result[SIDE:, at] - light[1] * result[:SIDE, at]) * 0.25
            col = cols[0, k]
            low = col >> 7
            wide = jnp.concatenate([contrib, jnp.zeros((SIDE, SIDE), F32)], axis=1)
            wide = pltpu.roll(wide, col & 127, 1).astype(BF)
            left = wide[:, :SIDE]
            right = wide[:, SIDE:]
            none = jnp.zeros((SIDE, SIDE), BF)
            for b in range(W // SIDE):
                placed[k * SIDE : (k + 1) * SIDE, b * SIDE : (b + 1) * SIDE] = jnp.where(
                    low == b, left, jnp.where(low + 1 == b, right, none)
                )

    def copy_s(n, i):
        return pltpu.make_async_remote_copy(
            src_ref=stage.at[n, i], dst_ref=from_x.at[n, i], send_sem=sxs.at[n, i], recv_sem=sxr.at[n, i],
            device_id=(a, at_x(i)), device_id_type=MESH,
        )

    def canvas_of(n, i):
        at = pl.ds(pl.multiple_of(lax.rem(x + i, TX) * rows_x, rows_x), rows_x)
        return jnp.dot(hot[at, :], placed[:, n * WIDE : (n + 1) * WIDE], preferred_element_type=F32)

    for n in range(CHUNKS):
        for i in (2, 1, 3):
            stage[n, i] = canvas_of(n, i).astype(BF)
            copy_s(n, i).start()
        mine[n] = canvas_of(n, 0)

    def copy_z(n, i):
        return pltpu.make_async_remote_copy(
            src_ref=part.at[n, lax.rem(z + i, TZ)], dst_ref=from_z.at[n, i],
            send_sem=szs.at[n, i], recv_sem=szr.at[n, i],
            device_id=(a, at_z(i)), device_id_type=MESH,
        )

    for n in range(CHUNKS):
        total = mine[n]
        for i in (1, 3, 2):
            copy_s(n, i).wait_recv()
            total = total + from_x[n, i].astype(F32)
        total = total.astype(BF)
        for j in range(TZ):
            part[n, j] = total[j * STRIP : (j + 1) * STRIP]
        for i in (4, 3, 5, 2, 6, 1, 7):
            copy_z(n, i).start()

    blocks = []
    for n in range(CHUNKS):
        strip = part[n, z].astype(F32)
        for i in (1, 7, 2, 6, 3, 5, 4):
            copy_z(n, i).wait_recv()
            strip = strip + from_z[n, i].astype(F32)
        strip = strip.astype(BF)
        blocks += [strip[:, c * 128 : (c + 1) * 128] for c in range(WIDE // 128)]
    picked = jnp.dot(
        sel[...].reshape(ANGLES * 16, 128), jnp.concatenate(blocks, axis=0), preferred_element_type=F32
    )
    pieces[...] = picked.astype(BF).reshape(ANGLES, 16, 128)

    def copy_a(i):
        peer = lax.rem(a + i, ANGLES)
        return pltpu.make_async_remote_copy(
            src_ref=pieces.at[peer], dst_ref=sino.at[a], send_sem=as_.at[i], recv_sem=ar.at[i],
            device_id=(peer, me), device_id_type=MESH,
        )

    def start_a(i, c):
        copy_a(i).start()
        return c

    lax.fori_loop(1, ANGLES, start_a, 0)
    sino[a] = pieces[a]

    for i in range(1, TZ):
        copy_ids(i).wait_send()
    for q in range(TZ):
        for i in range(1, TX):
            copy_x(q, i).wait_send()
    for c in range(4):
        for level in range(1, CHAINS[c][1] + 1):
            copy_chain(c, level).wait_send()
    for n in range(CHUNKS):
        for i in range(1, TX):
            copy_s(n, i).wait_send()
        for i in range(1, TZ):
            copy_z(n, i).wait_send()

    def finish_a(i, c):
        source = lax.rem(a - i + ANGLES, ANGLES)
        pltpu.make_async_remote_copy(
            src_ref=pieces.at[source], dst_ref=sino.at[source], send_sem=as_.at[i], recv_sem=ar.at[i],
            device_id=(source, me), device_id_type=MESH,
        ).wait_recv()
        return c

    lax.fori_loop(1, ANGLES, finish_a, 0)
    out[...] = sino[...]

    def sent_a(i, c):
        copy_a(i).wait_send()
        return c

    lax.fori_loop(1, ANGLES, sent_a, 0)


def shifted(values, step):
    if step == 0:
        return values
    lane = lax.broadcasted_iota(jnp.int32, values.shape, 1) + step
    rolled = pltpu.roll(values, (-step) % W, 1)
    return jnp.where((lane >= 0) & (lane < W), rolled, 0.0)


def slab_kernel(first, second, tangents, sino, out, flat, k_in, k_out):
    rows = SHIFTS * XW
    row = lax.broadcasted_iota(jnp.int32, (rows, ANGLES), 0)
    offset = (row % XW).astype(F32) - (XW - 1) / 2.0
    shift = (row // XW).astype(F32) - float(SPREAD)
    weight = jnp.maximum(1.0 - jnp.abs(offset * tangents[...] - shift), 0.0) * (1.0 / ANGLES)
    high = weight.astype(BF)
    low = (weight - high.astype(F32)).astype(BF)
    weights = jnp.concatenate([high, low], axis=1)

    r16 = lax.broadcasted_iota(jnp.int32, (XW, 128), 0)
    lane = lax.broadcasted_iota(jnp.int32, (XW, 128), 1)
    masks = [
        [((lane // XW == dj) & (lane % XW == r16 + di - 1)).astype(F32) for dj in range(3)] for di in range(3)
    ]
    for ch in range(CH):
        total = jnp.zeros((XW, 128), F32)
        for di in range(3):
            for dj in range(3):
                total = total + masks[di][dj] * first[ch, di * 3 + dj]
        k_in[ch * XW : (ch + 1) * XW, :] = total.astype(BF)
    near = [(lane % XW == r16 + di - 1) for di in range(3)]
    marks = [[(near[di] & (lane // XW == q)).astype(F32) for di in range(3)] for q in range(8)]
    for block in range(CH // 8):
        for dj in range(3):
            total = jnp.zeros((XW, 128), F32)
            for q in range(8):
                for di in range(3):
                    total = total + marks[q][di] * second[block * 8 + q, di * 3 + dj]
            k_out[dj * XW : (dj + 1) * XW, block * 128 : (block + 1) * 128] = total.astype(BF)

    flat[...] = sino[...].astype(F32).reshape(ANGLES * 16, 128)
    for r in range(2):
        rows_r = jnp.concatenate(
            [flat[pl.ds(2 * c + r, ANGLES, stride=16), :] for c in range(W // 128)], axis=1
        ).astype(BF)
        both = jnp.concatenate([rows_r, rows_r], axis=0)
        spread = jnp.dot(weights, both, preferred_element_type=F32)
        picture = jnp.zeros((XW, W), F32)
        for s in range(SHIFTS):
            picture = picture + shifted(spread[s * XW : (s + 1) * XW], s - SPREAD)
        rounded = picture.astype(BF).astype(F32)
        stack = jnp.concatenate([shifted(rounded, dj - 1) for dj in range(3)], axis=0).astype(BF)
        hidden = jnp.dot(k_in[:, : 3 * XW], stack, preferred_element_type=F32)
        hidden = jnp.maximum(hidden, 0.0).astype(BF)
        extra = jnp.dot(k_out[...], hidden, preferred_element_type=F32)
        for dj in range(3):
            picture = picture + shifted(extra[dj * XW : (dj + 1) * XW], dj - 1)
        out[r] = picture


def body(patches, magnitudes, probe, owners, scan_rows, scan_cols, slab_rows, angle_tan, prior_in, prior_out):
    vmem = pl.BlockSpec(memory_space=pltpu.VMEM)
    smem = pl.BlockSpec(memory_space=pltpu.SMEM)
    hbm = pl.BlockSpec(memory_space=pl.ANY)
    dma = pltpu.SemaphoreType.DMA
    numbers = dft_table(SIDE)
    table = jnp.asarray(numbers).astype(BF)
    table_t = jnp.asarray(np.ascontiguousarray(numbers.T)).astype(BF)
    rows_x = TZ * STRIP

    sino = pl.pallas_call(
        fused_kernel,
        out_shape=jax.ShapeDtypeStruct((ANGLES, 16, 128), BF),
        in_specs=[smem, smem, smem, smem, hbm, hbm, hbm, hbm, hbm],
        out_specs=vmem,
        scratch_shapes=[pltpu.VMEM((2 * TX, SIDE, SIDE), BF)] * TZ
        + [pltpu.VMEM((first + 1, HALF, SIDE, SIDE), BF) for _, first, _ in CHAINS]
        + [
            pltpu.VMEM((COUNT, 2, SIDE, SIDE), BF),
            pltpu.VMEM((2, SIDE, SIDE), F32),
            pltpu.VMEM((2 * SIDE, 2 * SIDE), BF),
            pltpu.VMEM((2 * SIDE, 2 * SIDE), BF),
            pltpu.VMEM((8, 128), jnp.int32),
            pltpu.VMEM((TZ, 8, 128), jnp.int32),
            pltpu.SMEM((TZ, 8, 128), jnp.int32),
            pltpu.VMEM((2 * SIDE, COUNT * SIDE), F32),
            pltpu.VMEM((H, COUNT * SIDE), BF),
            pltpu.VMEM((COUNT * SIDE, W), BF),
            pltpu.VMEM((CHUNKS, TX, rows_x, WIDE), BF),
            pltpu.VMEM((CHUNKS, TX, rows_x, WIDE), BF),
            pltpu.VMEM((CHUNKS, rows_x, WIDE), F32),
            pltpu.VMEM((CHUNKS, TZ, STRIP, WIDE), BF),
            pltpu.VMEM((CHUNKS, TZ, STRIP, WIDE), BF),
            pltpu.VMEM((ANGLES, 16, 128), BF),
            pltpu.VMEM((ANGLES, 16, 128), BF),
            pltpu.VMEM((ANGLES, 16, 128), BF),
            dma((12,)),
            dma((TZ, TX)),
            dma((TZ, TX)),
            dma((4, 5)),
            dma((4, 5)),
            dma((TZ,)),
            dma((TZ,)),
            dma,
            dma((CHUNKS, TX)),
            dma((CHUNKS, TX)),
            dma((CHUNKS, TZ)),
            dma((CHUNKS, TZ)),
            dma((ANGLES,)),
            dma((ANGLES,)),
        ],
        compiler_params=pltpu.CompilerParams(
            collective_id=0, has_side_effects=True, vmem_limit_bytes=60 * 1024 * 1024
        ),
        name="frames_to_slabs",
    )(
        owners.reshape(1, COUNT), scan_rows, scan_cols, slab_rows, patches[0], magnitudes[0], probe, table, table_t
    )

    volume = pl.pallas_call(
        slab_kernel,
        out_shape=jax.ShapeDtypeStruct((2, XW, W), F32),
        in_specs=[smem, smem, vmem, vmem],
        out_specs=vmem,
        scratch_shapes=[
            pltpu.VMEM((ANGLES * 16, 128), F32),
            pltpu.VMEM((CH * XW, 128), BF),
            pltpu.VMEM((3 * XW, CH * XW), BF),
        ],
        compiler_params=pltpu.CompilerParams(vmem_limit_bytes=48 * 1024 * 1024),
        name="slabs",
    )(
        prior_in.astype(F32).reshape(CH, 9),
        prior_out.astype(F32).reshape(CH, 9),
        angle_tan.reshape(1, ANGLES),
        sino,
    )
    return volume[None]


def solution(mesh):
    placed = (
        P("angle", "tile", None, None, None),
        P("angle", "tile", None, None),
        P(),
        P("angle", "tile", None),
        P("angle", "tile"),
        P("angle", "tile"),
        P("tile", None),
        P(),
        P(),
        P(),
    )
    return jax.shard_map(
        body, mesh=mesh, in_specs=placed, out_specs=P("tile", "angle", None, None), check_vma=False
    )
```

time: 106 us -> 76.7 us (0.72)
  Pallas kernels: 103 us -> 74.1 us
    pallas_call x3 -> x1, Pallas kernels: 99.7 us -> 71 us  [body(): pl.pallas_call(fused_kernel, out_shape=jax.ShapeDtypeStruct((ANGLES, 16,...]
    unnamed x24 -> x4, local copies, waits for them, and re-layouts: 2.32 us -> 0.84 us
where the time goes in v2:
time: 76.7 us; the launch traced here: 76.5 us
  Pallas kernels  74.1 us (97%)
  local copies, waits for them, and re-layouts  2.4 us (3%)
    pallas_call x1, Pallas kernels, body(): pl.pallas_call(fused_kernel, out_shape=jax.ShapeDtypeStruct((ANGLES, 16,...  71 us
    pallas_call x1, Pallas kernels, body(): pl.pallas_call(slab_kernel, out_shape=jax.ShapeDtypeStruct((2, XW, W), F3...  3.13 us

profile of v2, /device:TPU:1, one launch (start us, length us, event | category | flops | bytes accessed | tf_op | source)
XLA Modules:
  0.0 76.5 jit_solution(15902936224442565515)
XLA Ops:
  0.0 0.0 copy-start.1
  0.0 0.7 reshape.23
  0.7 0.1 copy.15.first
  0.8 0.7 reshape.25
  1.5 0.1 copy.16.second
  1.6 71.0 %frames_to_slabs.1.sino = bf16[16,16,128]{2,1,0:T(8,128)(2,1)} custom-call(s32[1,8]{1,0:T(1,128)} %bitcast.12, s32[1,8]{1,0:T(1,128)} %rows.1, s32[1,8]{1,0:T(1,128)} %cols.1, s32[1,16]{1,0:T(1,128)} %lengths.1, bf16[8,2,128,128]{3,2,1,0:T(8,128)(2,1)} %bitcast.11, bf16[64,128,128]{2,1,0:T(8,128)(2,1)} %bitcast.10, f32[2,128,128]{2,1,0:T(8,128)} %probe.1, ...), custom_call_target="tpu_custom_call" | custom-call | tf_op jit(solution)/shard_map/frames_to_slabs/pallas_call | solution.py:423
  72.5 0.0 copy-done.1
  72.6 0.0 copy-start
  72.6 0.8 %copy-done = bf16[16,16,128]{2,1,0:T(8,128)(2,1)S(1)} copy-done((bf16[16,16,128]{2,1,0:T(8,128)(2,1)S(1)}, bf16[16,16,128]{2,1,0:T(8,128)(2,1)}, u32[]{:S(2)}) %copy-start) | copy-done | bytes 65560
  73.4 3.1 %slabs.1 = f32[2,16,1024]{2,1,0:T(8,128)} custom-call(f32[16,9]{1,0:T(8,128)S(1)} %copy.15.first, f32[16,9]{1,0:T(8,128)S(1)} %copy.16.second, f32[1,16]{1,0:T(1,128)S(1)} %bitcast.9, bf16[16,16,128]{2,1,0:T(8,128)(2,1)S(1)} %copy-done), custom_call_target="tpu_custom_call" | custom-call | tf_op jit(solution)/shard_map/slabs/pallas_call | solution.py:472
Async XLA Ops:
  0.0 72.5 %copy-start.1 = (f32[16]{0:T(128)S(1)}, f32[16]{0:T(128)}, u32[]{:S(2)}) copy-start(f32[16]{0:T(128)} %param.19) | copy-start | bytes 196
  72.6 0.8 %copy-start = (bf16[16,16,128]{2,1,0:T(8,128)(2,1)S(1)}, bf16[16,16,128]{2,1,0:T(8,128)(2,1)}, u32[]{:S(2)}) copy-start(bf16[16,16,128]{2,1,0:T(8,128)(2,1)} %frames_to_slabs.1.sino) | copy-start | bytes 196612

commit v3 on v2

--- a/solution.py
+++ b/solution.py
@@ -1,3 +1,4 @@
+import functools
 import math
 
 import jax
@@ -22,10 +23,12 @@
 SPREAD = 4
 SHIFTS = 2 * SPREAD + 1
 HALF = COUNT // 2
-CHUNKS = 4
-WIDE = W // CHUNKS
-AHEAD = 3
-ORDER = (4, 3, -3, 2, -2, 1, -1, 0)
+CHUNKS = 3
+WIDE = W // (CHUNKS + 1)
+AHEAD = 6
+PARTS = 2
+LINES = SIDE // PARTS
+ORDER = ((4, 0), (4, 1), (3, 0), (-3, 0), (3, 1), (-3, 1), (2, 0), (-2, 0), (2, 1), (-2, 1), (1, 0), (-1, 0), (1, 1), (-1, 1), (0, 0), (0, 1))
 CHAINS = ((1, 4, 0), (-1, 3, 0), (1, 3, HALF), (-1, 4, HALF))
 MESH = pl.DeviceIdType.MESH
 BF = jnp.bfloat16
@@ -44,13 +47,22 @@
     return np.concatenate([upper, lower], axis=0).astype(np.float32)
 
 
+def shifted(values, step):
+    if step == 0:
+        return values
+    lane = lax.broadcasted_iota(jnp.int32, values.shape, 1) + step
+    rolled = pltpu.roll(values, (-step) % W, 1)
+    return jnp.where((lane >= 0) & (lane < W), rolled, 0.0)
+
+
 def fused_kernel(
-    owners, rows, cols, lengths, patches, mags, probe, table, table_t, out,
-    f0, f1, f2, f3, f4, f5, f6, f7, c0, c1, c2, c3,
-    waves, light, fwd, fwd_t, ids_out, ids_in, ids_s, spec, hot, placed, stage, from_x, mine, part, from_z, sel,
-    pieces, sino, loc, xs, xr, cs, cr, is_, ir, ls, sxs, sxr, szs, szr, as_, ar,
+    owners, rows, cols, lengths, tangents, patches, mags, probe, table, table_t, first, second, out,
+    f0, f1, f2, f3, f4, f5, f6, f7, f8, f9, f10, f11, f12, f13, f14, f15, c0, c1, c2, c3,
+    waves, light, fwd, fwd_t, one_in, one_out, ids_out, ids_in, ids_s, spec, hot, placed, stage, from_x, mine, part,
+    from_z, stage_b, from_zb, part_b, from_xb, sel, pieces, sino, flat, weights, k_in, k_out,
+    loc, xs, xr, cs, cr, is_, ir, ls, sxs, sxr, szs, szr, bzs, bzr, bxs, bxr, as_, ar,
 ):
-    frames = (f0, f1, f2, f3, f4, f5, f6, f7)
+    frames = (f0, f1, f2, f3, f4, f5, f6, f7, f8, f9, f10, f11, f12, f13, f14, f15)
     chains = (c0, c1, c2, c3)
     a = lax.axis_index("angle")
     me = lax.axis_index("tile")
@@ -65,10 +77,12 @@
         return x * TZ + lax.rem(z + i + TZ, TZ)
 
     local = [
-        pltpu.make_async_copy(patches, waves, loc.at[8]),
-        pltpu.make_async_copy(table, fwd, loc.at[9]),
-        pltpu.make_async_copy(table_t, fwd_t, loc.at[10]),
-        pltpu.make_async_copy(probe, light, loc.at[11]),
+        pltpu.make_async_copy(patches, waves, loc.at[16]),
+        pltpu.make_async_copy(table, fwd, loc.at[17]),
+        pltpu.make_async_copy(table_t, fwd_t, loc.at[18]),
+        pltpu.make_async_copy(probe, light, loc.at[19]),
+        pltpu.make_async_copy(first, one_in, loc.at[20]),
+        pltpu.make_async_copy(second, one_out, loc.at[21]),
     ]
     for copy in local:
         copy.start()
@@ -76,12 +90,16 @@
     def source_z(d):
         return lax.rem(z + d + TZ, TZ)
 
+    def held(q):
+        return frames[q].at[pl.ds(x * 2, 2)]
+
     def own_frames(q):
+        d, h = ORDER[q]
         return pltpu.make_async_copy(
-            mags.at[pl.ds((x * TZ + source_z(ORDER[q])) * 2, 2)], frames[q].at[pl.ds(x * 2, 2)], loc.at[q]
-        )
-
-    for q in range(TZ):
+            mags.at[pl.ds((x * TZ + source_z(d)) * 2, 2), pl.ds(h * LINES, LINES)], held(q), loc.at[q]
+        )
+
+    for q in range(len(ORDER)):
         own_frames(q).start()
 
     barrier = pltpu.get_barrier_semaphore()
@@ -114,10 +132,11 @@
         copy_ids(i).start()
 
     def copy_x(q, i):
+        d, h = ORDER[q]
         peer = at_x(i)
         return pltpu.make_async_remote_copy(
-            src_ref=mags.at[pl.ds(((peer // TZ) * TZ + source_z(ORDER[q])) * 2, 2)],
-            dst_ref=frames[q].at[pl.ds(x * 2, 2)],
+            src_ref=mags.at[pl.ds(((peer // TZ) * TZ + source_z(d)) * 2, 2), pl.ds(h * LINES, LINES)],
+            dst_ref=held(q),
             send_sem=xs.at[q, i], recv_sem=xr.at[q, i],
             device_id=(a, peer), device_id_type=MESH,
         )
@@ -168,6 +187,40 @@
             fwd_t[...], stack(half), preferred_element_type=F32
         )
 
+    count = SHIFTS * XW
+    row = lax.broadcasted_iota(jnp.int32, (count, ANGLES), 0)
+    offset = (row % XW).astype(F32) - (XW - 1) / 2.0
+    shift = (row // XW).astype(F32) - float(SPREAD)
+    angle_lane = lax.broadcasted_iota(jnp.int32, (count, ANGLES), 1)
+    tangent = jnp.zeros((count, ANGLES), F32)
+    for k in range(ANGLES):
+        tangent = jnp.where(angle_lane == k, tangents[k], tangent)
+    weight = jnp.maximum(1.0 - jnp.abs(offset * tangent - shift), 0.0) * (1.0 / ANGLES)
+    high = weight.astype(BF)
+    low = (weight - high.astype(F32)).astype(BF)
+    weights[...] = jnp.concatenate([high, low], axis=1)
+
+    channels = CH * XW
+    spread_ch = (
+        lax.broadcasted_iota(jnp.int32, (CH, channels), 1) // XW == lax.broadcasted_iota(jnp.int32, (CH, channels), 0)
+    )
+    spread_ch = spread_ch.astype(F32).astype(BF)
+    r16 = lax.broadcasted_iota(jnp.int32, (XW, channels), 0)
+    l16 = lax.broadcasted_iota(jnp.int32, (XW, channels), 1) % XW
+    first_taps = [jnp.dot(one_in[0, di], spread_ch, preferred_element_type=F32) for di in range(3)]
+    second_taps = [jnp.dot(one_out[0, di], spread_ch, preferred_element_type=F32) for di in range(3)]
+    turned = []
+    for dj in range(3):
+        total_in = jnp.zeros((XW, channels), F32)
+        total_out = jnp.zeros((XW, channels), F32)
+        for di in range(3):
+            total_in = total_in + jnp.where(r16 == l16 + di - 1, first_taps[di][dj : dj + 1, :], 0.0)
+            total_out = total_out + jnp.where(l16 == r16 + di - 1, second_taps[di][dj : dj + 1, :], 0.0)
+        turned.append(total_in)
+        k_out[dj * XW : (dj + 1) * XW, :] = total_out.astype(BF)
+    turned = jnp.concatenate(turned + [jnp.zeros((128 - 3 * XW, channels), F32)], axis=0)
+    k_in[...] = jnp.transpose(turned).astype(BF)
+
     for i in (1, 7, 2, 6, 3, 5, 4):
         copy_ids(i).wait_recv()
     to_scalar = pltpu.make_async_copy(ids_in, ids_s, ls)
@@ -175,7 +228,7 @@
     to_scalar.wait()
 
     def chosen(q):
-        d = ORDER[q]
+        d, h = ORDER[q]
         ids = mine_ids if d == 0 else [ids_s[(-d) % TZ, 0, k] for k in range(COUNT)]
 
         def one(k):
@@ -186,47 +239,52 @@
 
         return one
 
-    def copy_chain(c, level):
+    def copy_chain(c, h, level):
         step = CHAINS[c][0]
         return pltpu.make_async_remote_copy(
-            src_ref=chains[c].at[level], dst_ref=chains[c].at[level - 1],
-            send_sem=cs.at[c, level], recv_sem=cr.at[c, level - 1],
+            src_ref=chains[c].at[h, level], dst_ref=chains[c].at[h, level - 1],
+            send_sem=cs.at[c, h, level], recv_sem=cr.at[c, h, level - 1],
             device_id=(a, at_z(step)), device_id_type=MESH,
         )
 
-    for q in range(TZ):
-        if q + AHEAD < TZ:
+    for q in range(len(ORDER)):
+        if q + AHEAD < len(ORDER):
             start_x(q + AHEAD)
         own_frames(q).wait()
         for i in (1, 3, 2):
             copy_x(q, i).wait_recv()
+        d, h = ORDER[q]
+        if d == 0:
+            continue
         pick = chosen(q)
-        d = ORDER[q]
-        if d == 0:
-            for c in range(4):
-                copy_chain(c, 1).wait_recv()
-            break
         for c in range(4):
-            step, first, base = CHAINS[c]
+            step, top, base = CHAINS[c]
             level = 4 if d == 4 else step * d
-            if level < 1 or level > first:
+            if level < 1 or level > top:
                 continue
-            if level < first:
-                copy_chain(c, level + 1).wait_recv()
+            if level < top:
+                copy_chain(c, h, level + 1).wait_recv()
             for k in range(HALF):
                 hit, frame = pick(base + k)
-                before = chains[c][level, k] if level < first else jnp.zeros((SIDE, SIDE), BF)
-                chains[c][level, k] = jnp.where(hit, frame, before)
-            copy_chain(c, level).start()
+                before = chains[c][h, level, k] if level < top else jnp.zeros((LINES, SIDE), BF)
+                chains[c][h, level, k] = jnp.where(hit, frame, before)
+            copy_chain(c, h, level).start()
+    for h in range(PARTS):
+        for c in range(4):
+            copy_chain(c, h, 1).wait_recv()
+    picks = [chosen(ORDER.index((0, h))) for h in range(PARTS)]
 
     for g in range(COUNT // pair):
         ks = [g * pair + j for j in range(pair)]
         measured = []
         for k in ks:
-            hit, frame = pick(k)
             two = (0, 1) if k < HALF else (2, 3)
-            came = chains[two[0]][0, k % HALF] + chains[two[1]][0, k % HALF]
-            measured.append(jnp.where(hit, frame, came).astype(F32))
+            halves = []
+            for h in range(PARTS):
+                hit, frame = picks[h](k)
+                came = chains[two[0]][h, 0, k % HALF] + chains[two[1]][h, 0, k % HALF]
+                halves.append(jnp.where(hit, frame, came).astype(F32))
+            measured.append(jnp.concatenate(halves, axis=0))
         part_g = slice(g * pair * SIDE, (g + 1) * pair * SIDE)
         real = spec[:SIDE, part_g]
         imag = spec[SIDE:, part_g]
@@ -268,6 +326,25 @@
         at = pl.ds(pl.multiple_of(lax.rem(x + i, TX) * rows_x, rows_x), rows_x)
         return jnp.dot(hot[at, :], placed[:, n * WIDE : (n + 1) * WIDE], preferred_element_type=F32)
 
+    def copy_zb(i):
+        return pltpu.make_async_remote_copy(
+            src_ref=stage_b.at[lax.rem(z + i, TZ)], dst_ref=from_zb.at[i], send_sem=bzs.at[i], recv_sem=bzr.at[i],
+            device_id=(a, at_z(i)), device_id_type=MESH,
+        )
+
+    def copy_xb(i):
+        return pltpu.make_async_remote_copy(
+            src_ref=part_b.at[lax.rem(x + i, TX)], dst_ref=from_xb.at[i], send_sem=bxs.at[i], recv_sem=bxr.at[i],
+            device_id=(a, at_x(i)), device_id_type=MESH,
+        )
+
+    last = jnp.dot(hot[...], placed[:, CHUNKS * WIDE :], preferred_element_type=F32).astype(BF)
+    for j in range(TZ):
+        for k in range(TX):
+            stage_b[j, k] = last[(k * TZ + j) * STRIP : (k * TZ + j + 1) * STRIP]
+    for i in (4, 3, 5, 2, 6, 1, 7):
+        copy_zb(i).start()
+
     for n in range(CHUNKS):
         for i in (2, 1, 3):
             stage[n, i] = canvas_of(n, i).astype(BF)
@@ -291,13 +368,27 @@
             part[n, j] = total[j * STRIP : (j + 1) * STRIP]
         for i in (4, 3, 5, 2, 6, 1, 7):
             copy_z(n, i).start()
+        if n == 0:
+            total = stage_b[z].astype(F32)
+            for i in (1, 7, 2, 6, 3, 5, 4):
+                copy_zb(i).wait_recv()
+                total = total + from_zb[i].astype(F32)
+            part_b[...] = total.astype(BF)
+            for i in (2, 1, 3):
+                copy_xb(i).start()
 
     blocks = []
-    for n in range(CHUNKS):
-        strip = part[n, z].astype(F32)
-        for i in (1, 7, 2, 6, 3, 5, 4):
-            copy_z(n, i).wait_recv()
-            strip = strip + from_z[n, i].astype(F32)
+    for n in range(CHUNKS + 1):
+        if n < CHUNKS:
+            strip = part[n, z].astype(F32)
+            for i in (1, 7, 2, 6, 3, 5, 4):
+                copy_z(n, i).wait_recv()
+                strip = strip + from_z[n, i].astype(F32)
+        else:
+            strip = part_b[x].astype(F32)
+            for i in (1, 3, 2):
+                copy_xb(i).wait_recv()
+                strip = strip + from_xb[i].astype(F32)
         strip = strip.astype(BF)
         blocks += [strip[:, c * 128 : (c + 1) * 128] for c in range(WIDE // 128)]
     picked = jnp.dot(
@@ -321,12 +412,17 @@
 
     for i in range(1, TZ):
         copy_ids(i).wait_send()
-    for q in range(TZ):
+    for q in range(len(ORDER)):
         for i in range(1, TX):
             copy_x(q, i).wait_send()
     for c in range(4):
-        for level in range(1, CHAINS[c][1] + 1):
-            copy_chain(c, level).wait_send()
+        for h in range(PARTS):
+            for level in range(1, CHAINS[c][1] + 1):
+                copy_chain(c, h, level).wait_send()
+    for i in range(1, TZ):
+        copy_zb(i).wait_send()
+    for i in range(1, TX):
+        copy_xb(i).wait_send()
     for n in range(CHUNKS):
         for i in range(1, TX):
             copy_s(n, i).wait_send()
@@ -342,53 +438,12 @@
         return c
 
     lax.fori_loop(1, ANGLES, finish_a, 0)
-    out[...] = sino[...]
 
     def sent_a(i, c):
         copy_a(i).wait_send()
         return c
 
     lax.fori_loop(1, ANGLES, sent_a, 0)
-
-
-def shifted(values, step):
-    if step == 0:
-        return values
-    lane = lax.broadcasted_iota(jnp.int32, values.shape, 1) + step
-    rolled = pltpu.roll(values, (-step) % W, 1)
-    return jnp.where((lane >= 0) & (lane < W), rolled, 0.0)
-
-
-def slab_kernel(first, second, tangents, sino, out, flat, k_in, k_out):
-    rows = SHIFTS * XW
-    row = lax.broadcasted_iota(jnp.int32, (rows, ANGLES), 0)
-    offset = (row % XW).astype(F32) - (XW - 1) / 2.0
-    shift = (row // XW).astype(F32) - float(SPREAD)
-    weight = jnp.maximum(1.0 - jnp.abs(offset * tangents[...] - shift), 0.0) * (1.0 / ANGLES)
-    high = weight.astype(BF)
-    low = (weight - high.astype(F32)).astype(BF)
-    weights = jnp.concatenate([high, low], axis=1)
-
-    r16 = lax.broadcasted_iota(jnp.int32, (XW, 128), 0)
-    lane = lax.broadcasted_iota(jnp.int32, (XW, 128), 1)
-    masks = [
-        [((lane // XW == dj) & (lane % XW == r16 + di - 1)).astype(F32) for dj in range(3)] for di in range(3)
-    ]
-    for ch in range(CH):
-        total = jnp.zeros((XW, 128), F32)
-        for di in range(3):
-            for dj in range(3):
-                total = total + masks[di][dj] * first[ch, di * 3 + dj]
-        k_in[ch * XW : (ch + 1) * XW, :] = total.astype(BF)
-    near = [(lane % XW == r16 + di - 1) for di in range(3)]
-    marks = [[(near[di] & (lane // XW == q)).astype(F32) for di in range(3)] for q in range(8)]
-    for block in range(CH // 8):
-        for dj in range(3):
-            total = jnp.zeros((XW, 128), F32)
-            for q in range(8):
-                for di in range(3):
-                    total = total + marks[q][di] * second[block * 8 + q, di * 3 + dj]
-            k_out[dj * XW : (dj + 1) * XW, block * 128 : (block + 1) * 128] = total.astype(BF)
 
     flat[...] = sino[...].astype(F32).reshape(ANGLES * 16, 128)
     for r in range(2):
@@ -396,7 +451,7 @@
             [flat[pl.ds(2 * c + r, ANGLES, stride=16), :] for c in range(W // 128)], axis=1
         ).astype(BF)
         both = jnp.concatenate([rows_r, rows_r], axis=0)
-        spread = jnp.dot(weights, both, preferred_element_type=F32)
+        spread = jnp.dot(weights[...], both, preferred_element_type=F32)
         picture = jnp.zeros((XW, W), F32)
         for s in range(SHIFTS):
             picture = picture + shifted(spread[s * XW : (s + 1) * XW], s - SPREAD)
@@ -413,25 +468,28 @@
 def body(patches, magnitudes, probe, owners, scan_rows, scan_cols, slab_rows, angle_tan, prior_in, prior_out):
     vmem = pl.BlockSpec(memory_space=pltpu.VMEM)
     smem = pl.BlockSpec(memory_space=pltpu.SMEM)
-    hbm = pl.BlockSpec(memory_space=pl.ANY)
+    hbm = pl.BlockSpec(memory_space=pltpu.HBM)
     dma = pltpu.SemaphoreType.DMA
+    stay = functools.partial(pltpu.with_memory_space_constraint, memory_space=pltpu.HBM)
     numbers = dft_table(SIDE)
     table = jnp.asarray(numbers).astype(BF)
     table_t = jnp.asarray(np.ascontiguousarray(numbers.T)).astype(BF)
     rows_x = TZ * STRIP
 
-    sino = pl.pallas_call(
+    volume = pl.pallas_call(
         fused_kernel,
-        out_shape=jax.ShapeDtypeStruct((ANGLES, 16, 128), BF),
-        in_specs=[smem, smem, smem, smem, hbm, hbm, hbm, hbm, hbm],
+        out_shape=jax.ShapeDtypeStruct((2, XW, W), F32),
+        in_specs=[smem, smem, smem, smem, smem, hbm, hbm, hbm, hbm, hbm, hbm, hbm],
         out_specs=vmem,
-        scratch_shapes=[pltpu.VMEM((2 * TX, SIDE, SIDE), BF)] * TZ
-        + [pltpu.VMEM((first + 1, HALF, SIDE, SIDE), BF) for _, first, _ in CHAINS]
+        scratch_shapes=[pltpu.VMEM((2 * TX, LINES, SIDE), BF)] * (PARTS * TZ)
+        + [pltpu.VMEM((PARTS, top + 1, HALF, LINES, SIDE), BF) for _, top, _ in CHAINS]
         + [
             pltpu.VMEM((COUNT, 2, SIDE, SIDE), BF),
             pltpu.VMEM((2, SIDE, SIDE), F32),
             pltpu.VMEM((2 * SIDE, 2 * SIDE), BF),
             pltpu.VMEM((2 * SIDE, 2 * SIDE), BF),
+            pltpu.VMEM((1, 3, 3, CH), BF),
+            pltpu.VMEM((1, 3, 3, CH), BF),
             pltpu.VMEM((8, 128), jnp.int32),
             pltpu.VMEM((TZ, 8, 128), jnp.int32),
             pltpu.SMEM((TZ, 8, 128), jnp.int32),
@@ -443,14 +501,22 @@
             pltpu.VMEM((CHUNKS, rows_x, WIDE), F32),
             pltpu.VMEM((CHUNKS, TZ, STRIP, WIDE), BF),
             pltpu.VMEM((CHUNKS, TZ, STRIP, WIDE), BF),
+            pltpu.VMEM((TZ, TX, STRIP, WIDE), BF),
+            pltpu.VMEM((TZ, TX, STRIP, WIDE), BF),
+            pltpu.VMEM((TX, STRIP, WIDE), BF),
+            pltpu.VMEM((TX, STRIP, WIDE), BF),
             pltpu.VMEM((ANGLES, 16, 128), BF),
             pltpu.VMEM((ANGLES, 16, 128), BF),
             pltpu.VMEM((ANGLES, 16, 128), BF),
-            dma((12,)),
-            dma((TZ, TX)),
-            dma((TZ, TX)),
-            dma((4, 5)),
-            dma((4, 5)),
+            pltpu.VMEM((ANGLES * 16, 128), F32),
+            pltpu.VMEM((SHIFTS * XW, 2 * ANGLES), BF),
+            pltpu.VMEM((CH * XW, 128), BF),
+            pltpu.VMEM((3 * XW, CH * XW), BF),
+            dma((22,)),
+            dma((16, TX)),
+            dma((16, TX)),
+            dma((4, PARTS, 5)),
+            dma((4, PARTS, 5)),
             dma((TZ,)),
             dma((TZ,)),
             dma,
@@ -458,34 +524,21 @@
             dma((CHUNKS, TX)),
             dma((CHUNKS, TZ)),
             dma((CHUNKS, TZ)),
+            dma((TZ,)),
+            dma((TZ,)),
+            dma((TX,)),
+            dma((TX,)),
             dma((ANGLES,)),
             dma((ANGLES,)),
         ],
         compiler_params=pltpu.CompilerParams(
-            collective_id=0, has_side_effects=True, vmem_limit_bytes=60 * 1024 * 1024
+            collective_id=0, has_side_effects=True, vmem_limit_bytes=32 * 1024 * 1024
         ),
-        name="frames_to_slabs",
+        name="frames_to_volume",
     )(
-        owners.reshape(1, COUNT), scan_rows, scan_cols, slab_rows, patches[0], magnitudes[0], probe, table, table_t
-    )
-
-    volume = pl.pallas_call(
-        slab_kernel,
-        out_shape=jax.ShapeDtypeStruct((2, XW, W), F32),
-        in_specs=[smem, smem, vmem, vmem],
-        out_specs=vmem,
-        scratch_shapes=[
-            pltpu.VMEM((ANGLES * 16, 128), F32),
-            pltpu.VMEM((CH * XW, 128), BF),
-            pltpu.VMEM((3 * XW, CH * XW), BF),
-        ],
-        compiler_params=pltpu.CompilerParams(vmem_limit_bytes=48 * 1024 * 1024),
-        name="slabs",
-    )(
-        prior_in.astype(F32).reshape(CH, 9),
-        prior_out.astype(F32).reshape(CH, 9),
-        angle_tan.reshape(1, ANGLES),
-        sino,
+        stay(owners.reshape(1, COUNT)), stay(scan_rows), stay(scan_cols), stay(slab_rows), stay(angle_tan), stay(patches[0]), stay(magnitudes[0]),
+        stay(probe), stay(table), stay(table_t), stay(prior_in.transpose(1, 2, 3, 0)),
+        stay(prior_out.transpose(0, 2, 3, 1)),
     )
     return volume[None]
 

time: 76.7 us -> 70.1 us (0.914)
  Pallas kernels: 74.1 us -> 69.3 us
  local copies, waits for them, and re-layouts: 2.4 us -> 0.66 us
    pallas_call x2 -> x1, Pallas kernels: 74.1 us -> 69.3 us  [body(): pl.pallas_call(fused_kernel, out_shape=jax.ShapeDtypeStruct((2, XW, W), F...]
    reshape x4 -> x0, local copies, waits for them, and re-layouts: 1.57 us -> none  [the longest x2 0.79 us: body(): prior_in.astype(F32).reshape(CH, 9)]
where the time goes in v3:
time: 70.1 us; the launch traced here: 70 us
  Pallas kernels  69.3 us (99%)
    pallas_call x1, Pallas kernels, body(): pl.pallas_call(fused_kernel, out_shape=jax.ShapeDtypeStruct((2, XW, W), F...  69.3 us

profile of v3, /device:TPU:1, one launch (start us, length us, event | category | flops | bytes accessed | tf_op | source)
XLA Modules:
  0.0 70.0 jit_solution(6393728446534160836)
XLA Ops:
  0.0 69.3 %frames_to_volume.1 = f32[2,16,1024]{2,1,0:T(8,128)S(1)} custom-call(s32[1,8]{1,0:T(1,128)} %bitcast.11, s32[1,8]{1,0:T(1,128)} %rows.1, s32[1,8]{1,0:T(1,128)} %cols.1, s32[1,16]{1,0:T(1,128)} %lengths.1, f32[16]{0:T(128)} %tangents.1, bf16[8,2,128,128]{3,2,1,0:T(8,128)(2,1)} %bitcast.8, bf16[64,128,128]{2,1,0:T(8,128)(2,1)} %bitcast.7, ...), custom_call_target="tpu_custom_call" | custom-call | tf_op jit(solution)/shard_map/frames_to_volume/pallas_call | solution.py:479
  69.3 0.7 copy.14

commit v4 on v3

--- a/solution.py
+++ b/solution.py
@@ -23,13 +23,15 @@
 SPREAD = 4
 SHIFTS = 2 * SPREAD + 1
 HALF = COUNT // 2
-CHUNKS = 3
-WIDE = W // (CHUNKS + 1)
+TOP = TZ // 2
+CHUNKS = 2
+LAST = 256
+WIDE = (W - LAST) // CHUNKS
 AHEAD = 6
 PARTS = 2
 LINES = SIDE // PARTS
 ORDER = ((4, 0), (4, 1), (3, 0), (-3, 0), (3, 1), (-3, 1), (2, 0), (-2, 0), (2, 1), (-2, 1), (1, 0), (-1, 0), (1, 1), (-1, 1), (0, 0), (0, 1))
-CHAINS = ((1, 4, 0), (-1, 3, 0), (1, 3, HALF), (-1, 4, HALF))
+CHAINS = ((1, 0), (-1, HALF))
 MESH = pl.DeviceIdType.MESH
 BF = jnp.bfloat16
 F32 = jnp.float32
@@ -56,14 +58,14 @@
 
 
 def fused_kernel(
-    owners, rows, cols, lengths, tangents, patches, mags, probe, table, table_t, first, second, out,
-    f0, f1, f2, f3, f4, f5, f6, f7, f8, f9, f10, f11, f12, f13, f14, f15, c0, c1, c2, c3,
-    waves, light, fwd, fwd_t, one_in, one_out, ids_out, ids_in, ids_s, spec, hot, placed, stage, from_x, mine, part,
+    owners_in, rows_in, cols_in, lengths_in, tangents_in, patches, mags, probe, table, table_t, first, second, out,
+    f0, f1, f2, f3, f4, f5, f6, f7, f8, f9, f10, f11, f12, f13, f14, f15, c0, c1,
+    owners, rows, cols, lengths, tangents, waves, light, fwd, fwd_t, one_in, one_out, ids_out, ids_in, spec, hot, placed, stage, from_x, part,
     from_z, stage_b, from_zb, part_b, from_xb, sel, pieces, sino, flat, weights, k_in, k_out,
-    loc, xs, xr, cs, cr, is_, ir, ls, sxs, sxr, szs, szr, bzs, bzr, bxs, bxr, as_, ar,
+    loc, xs, xr, cs, cr, is_, ir, sxs, sxr, szs, szr, bzs, bzr, bxs, bxr, as_, ar,
 ):
     frames = (f0, f1, f2, f3, f4, f5, f6, f7, f8, f9, f10, f11, f12, f13, f14, f15)
-    chains = (c0, c1, c2, c3)
+    chains = (c0, c1)
     a = lax.axis_index("angle")
     me = lax.axis_index("tile")
     x = me // TZ
@@ -76,6 +78,28 @@
     def at_z(i):
         return x * TZ + lax.rem(z + i + TZ, TZ)
 
+    barrier = pltpu.get_barrier_semaphore()
+    for i in (2, 1, 3):
+        pl.semaphore_signal(barrier, inc=1, device_id=(a, at_x(i)), device_id_type=MESH)
+    for i in (4, 3, 5, 2, 6, 1, 7):
+        pl.semaphore_signal(barrier, inc=1, device_id=(a, at_z(i)), device_id_type=MESH)
+
+    def greet(i, c):
+        pl.semaphore_signal(barrier, inc=1, device_id=(lax.rem(a + i, ANGLES), me), device_id_type=MESH)
+        return c
+
+    lax.fori_loop(1, ANGLES, greet, 0)
+
+    small = [
+        pltpu.make_async_copy(a_ref, b_ref, loc.at[22 + n])
+        for n, (a_ref, b_ref) in enumerate(
+            (
+                (owners_in, owners), (rows_in, rows), (cols_in, cols), (lengths_in, lengths), (tangents_in, tangents),
+            )
+        )
+    ]
+    for copy in small:
+        copy.start()
     local = [
         pltpu.make_async_copy(patches, waves, loc.at[16]),
         pltpu.make_async_copy(table, fwd, loc.at[17]),
@@ -102,19 +126,15 @@
     for q in range(len(ORDER)):
         own_frames(q).start()
 
-    barrier = pltpu.get_barrier_semaphore()
-    for i in range(1, TX):
-        pl.semaphore_signal(barrier, inc=1, device_id=(a, at_x(i)), device_id_type=MESH)
-    for i in range(1, TZ):
-        pl.semaphore_signal(barrier, inc=1, device_id=(a, at_z(i)), device_id_type=MESH)
-
-    def greet(i, c):
-        pl.semaphore_signal(barrier, inc=1, device_id=(lax.rem(a + i, ANGLES), me), device_id_type=MESH)
-        return c
-
-    lax.fori_loop(1, ANGLES, greet, 0)
-
-    mine_ids = [owners[0, k] for k in range(COUNT)]
+    for copy in small:
+        copy.wait()
+    named = [owners[0, k] for k in range(COUNT)]
+    mine_ids = []
+    for k in range(COUNT):
+        rank = jnp.int32(0)
+        for j in range(k):
+            rank = rank + jnp.where(named[j] == named[k], 1, 0).astype(jnp.int32)
+        mine_ids.append((named[k] & 7) * 16 + ((named[k] >> 3) & 3) * 2 + (rank & 1))
     lane = lax.broadcasted_iota(jnp.int32, (8, 128), 1)
     vector = jnp.zeros((8, 128), jnp.int32)
     for k in range(COUNT):
@@ -147,21 +167,6 @@
 
     for q in range(AHEAD):
         start_x(q)
-
-    row_id = lax.broadcasted_iota(jnp.int32, (16, 128), 0)
-    lane_id = lax.broadcasted_iota(jnp.int32, (16, 128), 1)
-    within = row_id % 2
-    same = (row_id // 2) == (lane_id // 16)
-    place = lane_id % 16 - within
-    begin = jnp.int32(0)
-    for b in range(ANGLES):
-        length = lengths[0, b]
-        hit = same & (place == begin) & (within < length)
-        sel[b] = hit.astype(F32).astype(BF)
-        begin = begin + length
-    gap = lax.broadcasted_iota(jnp.int32, (H, 128), 0) - lax.broadcasted_iota(jnp.int32, (H, 128), 1)
-    for k in range(COUNT):
-        hot[:, k * SIDE : (k + 1) * SIDE] = (gap == rows[0, k]).astype(F32).astype(BF)
 
     pair = 2
 
@@ -176,73 +181,105 @@
             axis=0,
         )
 
-    for copy in local:
-        copy.wait()
-    for g in range(COUNT // pair):
-        joined = jnp.concatenate(
-            [jnp.concatenate([waves[k, 0], waves[k, 1]], axis=1) for k in range(g * pair, (g + 1) * pair)], axis=0
-        )
-        half = jnp.dot(joined, fwd[...], preferred_element_type=F32).astype(BF)
-        spec[:, g * pair * SIDE : (g + 1) * pair * SIDE] = jnp.dot(
-            fwd_t[...], stack(half), preferred_element_type=F32
-        )
-
-    count = SHIFTS * XW
-    row = lax.broadcasted_iota(jnp.int32, (count, ANGLES), 0)
-    offset = (row % XW).astype(F32) - (XW - 1) / 2.0
-    shift = (row // XW).astype(F32) - float(SPREAD)
-    angle_lane = lax.broadcasted_iota(jnp.int32, (count, ANGLES), 1)
-    tangent = jnp.zeros((count, ANGLES), F32)
-    for k in range(ANGLES):
-        tangent = jnp.where(angle_lane == k, tangents[k], tangent)
-    weight = jnp.maximum(1.0 - jnp.abs(offset * tangent - shift), 0.0) * (1.0 / ANGLES)
-    high = weight.astype(BF)
-    low = (weight - high.astype(F32)).astype(BF)
-    weights[...] = jnp.concatenate([high, low], axis=1)
-
-    channels = CH * XW
-    spread_ch = (
-        lax.broadcasted_iota(jnp.int32, (CH, channels), 1) // XW == lax.broadcasted_iota(jnp.int32, (CH, channels), 0)
-    )
-    spread_ch = spread_ch.astype(F32).astype(BF)
-    r16 = lax.broadcasted_iota(jnp.int32, (XW, channels), 0)
-    l16 = lax.broadcasted_iota(jnp.int32, (XW, channels), 1) % XW
-    first_taps = [jnp.dot(one_in[0, di], spread_ch, preferred_element_type=F32) for di in range(3)]
-    second_taps = [jnp.dot(one_out[0, di], spread_ch, preferred_element_type=F32) for di in range(3)]
-    turned = []
-    for dj in range(3):
-        total_in = jnp.zeros((XW, channels), F32)
-        total_out = jnp.zeros((XW, channels), F32)
-        for di in range(3):
-            total_in = total_in + jnp.where(r16 == l16 + di - 1, first_taps[di][dj : dj + 1, :], 0.0)
-            total_out = total_out + jnp.where(l16 == r16 + di - 1, second_taps[di][dj : dj + 1, :], 0.0)
-        turned.append(total_in)
-        k_out[dj * XW : (dj + 1) * XW, :] = total_out.astype(BF)
-    turned = jnp.concatenate(turned + [jnp.zeros((128 - 3 * XW, channels), F32)], axis=0)
-    k_in[...] = jnp.transpose(turned).astype(BF)
-
-    for i in (1, 7, 2, 6, 3, 5, 4):
-        copy_ids(i).wait_recv()
-    to_scalar = pltpu.make_async_copy(ids_in, ids_s, ls)
-    to_scalar.start()
-    to_scalar.wait()
+    def slab_rows_of():
+        row_id = lax.broadcasted_iota(jnp.int32, (16, 128), 0)
+        lane_id = lax.broadcasted_iota(jnp.int32, (16, 128), 1)
+        within = row_id % 2
+        same = (row_id // 2) == (lane_id // 16)
+        place = lane_id % 16 - within
+        begin = jnp.int32(0)
+        for b in range(ANGLES):
+            length = lengths[0, b]
+            hit = same & (place == begin) & (within < length)
+            sel[b] = hit.astype(F32).astype(BF)
+            begin = begin + length
+
+    def row_places(ks):
+        gap = lax.broadcasted_iota(jnp.int32, (H, 128), 0) - lax.broadcasted_iota(jnp.int32, (H, 128), 1)
+        for k in ks:
+            hot[:, k * SIDE : (k + 1) * SIDE] = (gap == rows[0, k]).astype(F32).astype(BF)
+
+    def forward(gs):
+        for g in gs:
+            joined = jnp.concatenate(
+                [jnp.concatenate([waves[k, 0], waves[k, 1]], axis=1) for k in range(g * pair, (g + 1) * pair)], axis=0
+            )
+            half = jnp.dot(joined, fwd[...], preferred_element_type=F32).astype(BF)
+            spec[:, g * pair * SIDE : (g + 1) * pair * SIDE] = jnp.dot(
+                fwd_t[...], stack(half), preferred_element_type=F32
+            )
+
+    def matrices():
+        count = SHIFTS * XW
+        row = lax.broadcasted_iota(jnp.int32, (count, ANGLES), 0)
+        offset = (row % XW).astype(F32) - (XW - 1) / 2.0
+        shift = (row // XW).astype(F32) - float(SPREAD)
+        angle_lane = lax.broadcasted_iota(jnp.int32, (count, ANGLES), 1)
+        tangent = jnp.zeros((count, ANGLES), F32)
+        for k in range(ANGLES):
+            tangent = jnp.where(angle_lane == k, tangents[k], tangent)
+        weight = jnp.maximum(1.0 - jnp.abs(offset * tangent - shift), 0.0) * (1.0 / ANGLES)
+        high = weight.astype(BF)
+        low = (weight - high.astype(F32)).astype(BF)
+        weights[...] = jnp.concatenate([high, low], axis=1)
+
+        channels = CH * XW
+        spread_ch = (
+            lax.broadcasted_iota(jnp.int32, (CH, channels), 1) // XW == lax.broadcasted_iota(jnp.int32, (CH, channels), 0)
+        )
+        spread_ch = spread_ch.astype(F32).astype(BF)
+        r16 = lax.broadcasted_iota(jnp.int32, (XW, channels), 0)
+        l16 = lax.broadcasted_iota(jnp.int32, (XW, channels), 1) % XW
+        first_taps = [jnp.dot(one_in[0, di], spread_ch, preferred_element_type=F32) for di in range(3)]
+        second_taps = [jnp.dot(one_out[0, di], spread_ch, preferred_element_type=F32) for di in range(3)]
+        turned = []
+        for dj in range(3):
+            total_in = jnp.zeros((XW, channels), F32)
+            total_out = jnp.zeros((XW, channels), F32)
+            for di in range(3):
+                total_in = total_in + jnp.where(r16 == l16 + di - 1, first_taps[di][dj : dj + 1, :], 0.0)
+                total_out = total_out + jnp.where(l16 == r16 + di - 1, second_taps[di][dj : dj + 1, :], 0.0)
+            turned.append(total_in)
+            k_out[dj * XW : (dj + 1) * XW, :] = total_out.astype(BF)
+        turned = jnp.concatenate(turned + [jnp.zeros((128 - 3 * XW, channels), F32)], axis=0)
+        k_in[...] = jnp.transpose(turned).astype(BF)
+
+    def job(q):
+        if q == 1:
+            for copy in local:
+                copy.wait()
+            forward((0, 1))
+        elif q == 3:
+            forward((2, 3))
+        elif q == 5:
+            row_places(range(HALF))
+        elif q == 7:
+            row_places(range(HALF, COUNT))
+        elif q == 9:
+            matrices()
+        elif q == 11:
+            slab_rows_of()
+
+    known = {0: mine_ids}
 
     def chosen(q):
         d, h = ORDER[q]
-        ids = mine_ids if d == 0 else [ids_s[(-d) % TZ, 0, k] for k in range(COUNT)]
+        if d not in known:
+            came = (-d) % TZ
+            copy_ids(came).wait_recv()
+            known[d] = [ids_in[came, 0, k] for k in range(COUNT)]
+        ids = known[d]
 
         def one(k):
-            rank = jnp.int32(0)
-            for j in range(k):
-                rank = rank + jnp.where(ids[j] == ids[k], 1, 0).astype(jnp.int32)
-            return (ids[k] & 7) == z, frames[q][((ids[k] >> 3) & 3) * 2 + (rank & 1)]
+            return (ids[k] >> 4) == z, frames[q][ids[k] & 7]
 
         return one
 
     def copy_chain(c, h, level):
-        step = CHAINS[c][0]
-        return pltpu.make_async_remote_copy(
-            src_ref=chains[c].at[h, level], dst_ref=chains[c].at[h, level - 1],
+        step, base = CHAINS[c]
+        at = pl.ds(base, HALF) if level == TOP else pl.ds(0, COUNT)
+        return pltpu.make_async_remote_copy(
+            src_ref=chains[c].at[h, level, at], dst_ref=chains[c].at[h, level - 1, at],
             send_sem=cs.at[c, h, level], recv_sem=cr.at[c, h, level - 1],
             device_id=(a, at_z(step)), device_id_type=MESH,
         )
@@ -257,20 +294,25 @@
         if d == 0:
             continue
         pick = chosen(q)
-        for c in range(4):
-            step, top, base = CHAINS[c]
-            level = 4 if d == 4 else step * d
-            if level < 1 or level > top:
+        for c in range(2):
+            step, base = CHAINS[c]
+            level = TOP if d == TOP else step * d
+            if level < 1:
                 continue
-            if level < top:
+            if level < TOP:
                 copy_chain(c, h, level + 1).wait_recv()
-            for k in range(HALF):
-                hit, frame = pick(base + k)
-                before = chains[c][h, level, k] if level < top else jnp.zeros((LINES, SIDE), BF)
+            for k in range(COUNT):
+                here = base <= k < base + HALF
+                if level == TOP and not here:
+                    continue
+                hit, frame = pick(k)
+                came = level < TOP - 1 or (level == TOP - 1 and here)
+                before = chains[c][h, level, k] if came else jnp.zeros((LINES, SIDE), BF)
                 chains[c][h, level, k] = jnp.where(hit, frame, before)
             copy_chain(c, h, level).start()
+        job(q)
     for h in range(PARTS):
-        for c in range(4):
+        for c in range(2):
             copy_chain(c, h, 1).wait_recv()
     picks = [chosen(ORDER.index((0, h))) for h in range(PARTS)]
 
@@ -278,11 +320,10 @@
         ks = [g * pair + j for j in range(pair)]
         measured = []
         for k in ks:
-            two = (0, 1) if k < HALF else (2, 3)
             halves = []
             for h in range(PARTS):
                 hit, frame = picks[h](k)
-                came = chains[two[0]][h, 0, k % HALF] + chains[two[1]][h, 0, k % HALF]
+                came = chains[0][h, 0, k] + chains[1][h, 0, k]
                 halves.append(jnp.where(hit, frame, came).astype(F32))
             measured.append(jnp.concatenate(halves, axis=0))
         part_g = slice(g * pair * SIDE, (g + 1) * pair * SIDE)
@@ -318,13 +359,13 @@
 
     def copy_s(n, i):
         return pltpu.make_async_remote_copy(
-            src_ref=stage.at[n, i], dst_ref=from_x.at[n, i], send_sem=sxs.at[n, i], recv_sem=sxr.at[n, i],
+            src_ref=stage.at[n, lax.rem(x + i, TX)], dst_ref=from_x.at[n, i],
+            send_sem=sxs.at[n, i], recv_sem=sxr.at[n, i],
             device_id=(a, at_x(i)), device_id_type=MESH,
         )
 
-    def canvas_of(n, i):
-        at = pl.ds(pl.multiple_of(lax.rem(x + i, TX) * rows_x, rows_x), rows_x)
-        return jnp.dot(hot[at, :], placed[:, n * WIDE : (n + 1) * WIDE], preferred_element_type=F32)
+    def canvas_of(n):
+        return jnp.dot(hot[...], placed[:, n * WIDE : min(n * WIDE + WIDE, W)], preferred_element_type=F32).astype(BF)
 
     def copy_zb(i):
         return pltpu.make_async_remote_copy(
@@ -338,7 +379,7 @@
             device_id=(a, at_x(i)), device_id_type=MESH,
         )
 
-    last = jnp.dot(hot[...], placed[:, CHUNKS * WIDE :], preferred_element_type=F32).astype(BF)
+    last = canvas_of(CHUNKS)
     for j in range(TZ):
         for k in range(TX):
             stage_b[j, k] = last[(k * TZ + j) * STRIP : (k * TZ + j + 1) * STRIP]
@@ -346,10 +387,11 @@
         copy_zb(i).start()
 
     for n in range(CHUNKS):
+        whole = canvas_of(n)
+        for j in range(TX):
+            stage[n, j] = whole[j * rows_x : (j + 1) * rows_x]
         for i in (2, 1, 3):
-            stage[n, i] = canvas_of(n, i).astype(BF)
             copy_s(n, i).start()
-        mine[n] = canvas_of(n, 0)
 
     def copy_z(n, i):
         return pltpu.make_async_remote_copy(
@@ -359,7 +401,7 @@
         )
 
     for n in range(CHUNKS):
-        total = mine[n]
+        total = stage[n, x].astype(F32)
         for i in (1, 3, 2):
             copy_s(n, i).wait_recv()
             total = total + from_x[n, i].astype(F32)
@@ -390,7 +432,7 @@
                 copy_xb(i).wait_recv()
                 strip = strip + from_xb[i].astype(F32)
         strip = strip.astype(BF)
-        blocks += [strip[:, c * 128 : (c + 1) * 128] for c in range(WIDE // 128)]
+        blocks += [strip[:, c * 128 : (c + 1) * 128] for c in range(strip.shape[1] // 128)]
     picked = jnp.dot(
         sel[...].reshape(ANGLES * 16, 128), jnp.concatenate(blocks, axis=0), preferred_element_type=F32
     )
@@ -415,9 +457,9 @@
     for q in range(len(ORDER)):
         for i in range(1, TX):
             copy_x(q, i).wait_send()
-    for c in range(4):
+    for c in range(2):
         for h in range(PARTS):
-            for level in range(1, CHAINS[c][1] + 1):
+            for level in range(1, TOP + 1):
                 copy_chain(c, h, level).wait_send()
     for i in range(1, TZ):
         copy_zb(i).wait_send()
@@ -438,12 +480,6 @@
         return c
 
     lax.fori_loop(1, ANGLES, finish_a, 0)
-
-    def sent_a(i, c):
-        copy_a(i).wait_send()
-        return c
-
-    lax.fori_loop(1, ANGLES, sent_a, 0)
 
     flat[...] = sino[...].astype(F32).reshape(ANGLES * 16, 128)
     for r in range(2):
@@ -464,10 +500,15 @@
             picture = picture + shifted(extra[dj * XW : (dj + 1) * XW], dj - 1)
         out[r] = picture
 
+    def sent_a(i, c):
+        copy_a(i).wait_send()
+        return c
+
+    lax.fori_loop(1, ANGLES, sent_a, 0)
+
 
 def body(patches, magnitudes, probe, owners, scan_rows, scan_cols, slab_rows, angle_tan, prior_in, prior_out):
     vmem = pl.BlockSpec(memory_space=pltpu.VMEM)
-    smem = pl.BlockSpec(memory_space=pltpu.SMEM)
     hbm = pl.BlockSpec(memory_space=pltpu.HBM)
     dma = pltpu.SemaphoreType.DMA
     stay = functools.partial(pltpu.with_memory_space_constraint, memory_space=pltpu.HBM)
@@ -479,11 +520,16 @@
     volume = pl.pallas_call(
         fused_kernel,
         out_shape=jax.ShapeDtypeStruct((2, XW, W), F32),
-        in_specs=[smem, smem, smem, smem, smem, hbm, hbm, hbm, hbm, hbm, hbm, hbm],
+        in_specs=[hbm, hbm, hbm, hbm, hbm, hbm, hbm, hbm, hbm, hbm, hbm, hbm],
         out_specs=vmem,
         scratch_shapes=[pltpu.VMEM((2 * TX, LINES, SIDE), BF)] * (PARTS * TZ)
-        + [pltpu.VMEM((PARTS, top + 1, HALF, LINES, SIDE), BF) for _, top, _ in CHAINS]
+        + [pltpu.VMEM((PARTS, TOP + 1, COUNT, LINES, SIDE), BF)] * 2
         + [
+            pltpu.SMEM((1, COUNT), jnp.int32),
+            pltpu.SMEM((1, COUNT), jnp.int32),
+            pltpu.SMEM((1, COUNT), jnp.int32),
+            pltpu.SMEM((1, ANGLES), jnp.int32),
+            pltpu.SMEM((ANGLES,), F32),
             pltpu.VMEM((COUNT, 2, SIDE, SIDE), BF),
             pltpu.VMEM((2, SIDE, SIDE), F32),
             pltpu.VMEM((2 * SIDE, 2 * SIDE), BF),
@@ -492,19 +538,17 @@
             pltpu.VMEM((1, 3, 3, CH), BF),
             pltpu.VMEM((8, 128), jnp.int32),
             pltpu.VMEM((TZ, 8, 128), jnp.int32),
-            pltpu.SMEM((TZ, 8, 128), jnp.int32),
             pltpu.VMEM((2 * SIDE, COUNT * SIDE), F32),
             pltpu.VMEM((H, COUNT * SIDE), BF),
             pltpu.VMEM((COUNT * SIDE, W), BF),
             pltpu.VMEM((CHUNKS, TX, rows_x, WIDE), BF),
             pltpu.VMEM((CHUNKS, TX, rows_x, WIDE), BF),
-            pltpu.VMEM((CHUNKS, rows_x, WIDE), F32),
             pltpu.VMEM((CHUNKS, TZ, STRIP, WIDE), BF),
             pltpu.VMEM((CHUNKS, TZ, STRIP, WIDE), BF),
-            pltpu.VMEM((TZ, TX, STRIP, WIDE), BF),
-            pltpu.VMEM((TZ, TX, STRIP, WIDE), BF),
-            pltpu.VMEM((TX, STRIP, WIDE), BF),
-            pltpu.VMEM((TX, STRIP, WIDE), BF),
+            pltpu.VMEM((TZ, TX, STRIP, LAST), BF),
+            pltpu.VMEM((TZ, TX, STRIP, LAST), BF),
+            pltpu.VMEM((TX, STRIP, LAST), BF),
+            pltpu.VMEM((TX, STRIP, LAST), BF),
             pltpu.VMEM((ANGLES, 16, 128), BF),
             pltpu.VMEM((ANGLES, 16, 128), BF),
             pltpu.VMEM((ANGLES, 16, 128), BF),
@@ -512,14 +556,13 @@
             pltpu.VMEM((SHIFTS * XW, 2 * ANGLES), BF),
             pltpu.VMEM((CH * XW, 128), BF),
             pltpu.VMEM((3 * XW, CH * XW), BF),
-            dma((22,)),
+            dma((27,)),
             dma((16, TX)),
             dma((16, TX)),
-            dma((4, PARTS, 5)),
-            dma((4, PARTS, 5)),
+            dma((2, PARTS, TOP + 1)),
+            dma((2, PARTS, TOP + 1)),
             dma((TZ,)),
             dma((TZ,)),
-            dma,
             dma((CHUNKS, TX)),
             dma((CHUNKS, TX)),
             dma((CHUNKS, TZ)),

time: 70.1 us -> 69 us (0.984)
  Pallas kernels: 69.3 us -> 68.2 us
    pallas_call x1, Pallas kernels: 69.3 us -> 68.2 us  [body(): pl.pallas_call(fused_kernel, out_shape=jax.ShapeDtypeStruct((2, XW, W), F...]
where the time goes in v4:
time: 69 us; the launch traced here: 68.9 us
  Pallas kernels  68.2 us (99%)
    pallas_call x1, Pallas kernels, body(): pl.pallas_call(fused_kernel, out_shape=jax.ShapeDtypeStruct((2, XW, W), F...  68.2 us

profile of v4, /device:TPU:1, one launch (start us, length us, event | category | flops | bytes accessed | tf_op | source)
XLA Modules:
  0.0 68.9 jit_solution(10861749817805318978)
XLA Ops:
  0.0 68.2 %frames_to_volume.1 = f32[2,16,1024]{2,1,0:T(8,128)S(1)} custom-call(s32[1,8]{1,0:T(1,128)} %bitcast.11, s32[1,8]{1,0:T(1,128)} %rows_in.1, s32[1,8]{1,0:T(1,128)} %cols_in.1, s32[1,16]{1,0:T(1,128)} %lengths_in.1, f32[16]{0:T(128)} %tangents_in.1, bf16[8,2,128,128]{3,2,1,0:T(8,128)(2,1)} %bitcast.8, bf16[64,128,128]{2,1,0:T(8,128)(2,1)} %bitcast.7, ...), custom_call_target="tpu_custom_call" | custom-call | tf_op jit(solution)/shard_map/frames_to_volume/pallas_call | solution.py:520
  68.2 0.7 copy.14
